TPU v7x, 32 devices: a whole 2x2x4 slice. The times are simulated.
32 devices in a mesh: grp: 4 (over y, x), tile: 8 (over z, core).
Axes of the slice: x: 2, y: 2, z: 4, core: 2. Of those that a mesh axis runs over, the one named last changes fastest.
Arguments:
- ocean: float32 [4, 32, 16, 1024], P(None, None, 'grp', 'tile'), may hold values from -3 to 3
- tracers: bfloat16 [10, 32, 16, 1024], P(None, None, 'grp', 'tile'), may hold values from -6 to 6
- wet_blocks: int32 [4, 64], P('grp', 'tile'), may hold values 0 or 1
- surface_light: float32 [16, 1024], P('grp', 'tile'), may hold values from 0.5 to 1.5
- rates: float32 [10, 10], replicated, may hold values from -2 to 2
Outputs:
- ocean_out: float32 [4, 32, 16, 1024], P(None, None, 'grp', 'tile')
- tracer_out: bfloat16 [10, 32, 16, 1024], P(None, None, 'grp', 'tile')
- heating: float32 [32, 16, 1024], P(None, 'grp', 'tile')
All inputs are finite; a program needn't handle non-finite values. No bound on the sum of `wet_blocks` on one device may be relied on, other than what follows from the above.
Results may differ from a plain program's by a relative error of at most 0.0031.
Values may be sent and summed in bfloat16 or wider, within the bound.
A program may use at most 64 MiB of HBM per device.

v0:
```python
import jax
import jax.numpy as jnp
from jax import lax
from jax.sharding import PartitionSpec as P

WBY = 4
WBX = 16


time_step = 0.3
coriolis = 0.2
viscosity = 0.1
diffusion = 0.05
thermal = 0.2
haline = 0.15
gravity_red = 0.05
react_step = 0.5
water_atten = 0.3
chloro_atten = 0.2


def extended(array, sides, width):
    for axis, dim in sides:
        devices, length = (lax.axis_size(axis), array.shape[dim])
        up = [(i, (i + 1) % devices) for i in range(devices - 1)]
        down = [(j, i) for i, j in up]
        last = lax.slice_in_dim(array, length - width, length, axis=dim)
        first = lax.slice_in_dim(array, 0, width, axis=dim)
        before = lax.ppermute(last, axis, up)
        after = lax.ppermute(first, axis, down)
        array = jnp.concatenate([before, array, after], axis=dim)
    return array


def minmod(first, second):
    return 0.5 * (jnp.sign(first) + jnp.sign(second)) * jnp.minimum(jnp.abs(first), jnp.abs(second))


def ocean_tendency(padded):
    center = padded[:, :, 2:-2, 2:-2]
    east_side = padded[:, :, 2:-2, 3:-1]
    west_side = padded[:, :, 2:-2, 1:-3]
    north_side = padded[:, :, 3:-1, 2:-2]
    south_side = padded[:, :, 1:-3, 2:-2]
    grad_x = 0.5 * (east_side - west_side)
    grad_y = 0.5 * (north_side - south_side)
    laplace = east_side + west_side + north_side + south_side - 4.0 * center
    zonal_vel = center[0]
    merid_vel = center[1]
    advect = -(zonal_vel[None] * grad_x + merid_vel[None] * grad_y)
    press_x = gravity_red * jnp.cumsum(thermal * grad_x[2] - haline * grad_x[3], axis=0)
    press_y = gravity_red * jnp.cumsum(thermal * grad_y[2] - haline * grad_y[3], axis=0)
    zonal_rate = advect[0] + coriolis * merid_vel - press_x + viscosity * laplace[0]
    merid_rate = advect[1] - coriolis * zonal_vel - press_y + viscosity * laplace[1]
    heat_rate = advect[2] + diffusion * laplace[2]
    salt_rate = advect[3] + diffusion * laplace[3]
    return jnp.stack([zonal_rate, merid_rate, heat_rate, salt_rate], 0)


def limited_divergence(cells, speeds, axis):
    count = cells.shape[axis] - 4

    def part(source, start, length):
        return lax.slice_in_dim(source, start, start + length, axis=axis)

    face_speed = 0.5 * (part(speeds, 1, count + 1) + part(speeds, 2, count + 1))
    behind = part(cells, 0, count + 1)
    inside = part(cells, 1, count + 1)
    ahead = part(cells, 2, count + 1)
    beyond = part(cells, 3, count + 1)
    left_value = inside + 0.5 * minmod(inside - behind, ahead - inside)
    right_value = ahead - 0.5 * minmod(ahead - inside, beyond - ahead)
    flux = jnp.maximum(face_speed, 0.0) * left_value + jnp.minimum(face_speed, 0.0) * right_value
    return part(flux, 1, count) - part(flux, 0, count)


def tracer_tendency(cells, padded_ocean):
    zonal_row = padded_ocean[0:1, :, 2:-2, :]
    merid_col = padded_ocean[1:2, :, :, 2:-2]
    along_x = limited_divergence(cells[:, :, 2:-2, :], zonal_row, 3)
    along_y = limited_divergence(cells[:, :, :, 2:-2], merid_col, 2)
    return -(along_x + along_y)


def expand_mask(wet_blocks):
    blocks = wet_blocks.astype(jnp.float32)
    rows, cols = blocks.shape
    wide = jnp.broadcast_to(blocks[:, None, :, None], (rows, WBY, cols, WBX))
    return wide.reshape(rows * WBY, cols * WBX)


def section_rims(ocean_state, tracer_state):
    padded_ocean = extended(ocean_state, (("grp", 2), ("tile", 3)), 2)
    padded_tracer = extended(tracer_state, (("grp", 2), ("tile", 3)), 2).astype(jnp.float32)
    return (ocean_tendency(padded_ocean), tracer_tendency(padded_tracer, padded_ocean))


def shards(ocean, tracers, wet_blocks, surface_light, rates):
    start = tracers.astype(jnp.float32)
    ocean_rate, tracer_rate = section_rims(ocean, tracers)
    ocean_one = ocean + time_step * ocean_rate
    tracer_one = lax.optimization_barrier((start + time_step * tracer_rate).astype(jnp.bfloat16))
    ocean_rate, tracer_rate = section_rims(ocean_one, tracer_one)
    tracer_mid = tracer_one.astype(jnp.float32)
    ocean_two = 0.5 * (ocean + ocean_one + time_step * ocean_rate)
    tracer_two = 0.5 * (start + tracer_mid + time_step * tracer_rate)
    wet_cells = expand_mask(wet_blocks)
    reaction = jnp.einsum("ab,bzyx->azyx", rates, tracer_two, precision=lax.Precision.HIGHEST)
    reacted = tracer_two + react_step * wet_cells * reaction
    attenuation = water_atten + chloro_atten * reacted[0] * reacted[0]
    depth_sum = jnp.cumsum(attenuation, axis=0)
    heating = wet_cells * surface_light * (jnp.exp(attenuation - depth_sum) - jnp.exp(-depth_sum))
    ocean_out = jnp.concatenate(
        [ocean_two[:2], ocean_two[2:3] + time_step * heating[None], ocean_two[3:]], 0
    )
    return (ocean_out, reacted.astype(jnp.bfloat16), heating)


def solution(mesh):
    return jax.shard_map(
        shards,
        mesh=mesh,
        in_specs=(
            P(None, None, "grp", "tile"),
            P(None, None, "grp", "tile"),
            P("grp", "tile"),
            P("grp", "tile"),
            P(),
        ),
        out_specs=(
            P(None, None, "grp", "tile"),
            P(None, None, "grp", "tile"),
            P(None, "grp", "tile"),
        ),
        check_vma=False,
    )
```

profile of v0, /device:TPU:20, one launch (start us, length us, event | category | flops | bytes accessed | tf_op | source)
XLA Modules:
  0.0 90.0 jit_solution(14366851366576069977)
XLA Ops:
  1.7 3.5 %collective-permute-start.1 = (f32[4,32,2,128]{3,1,2,0:T(8,128)S(1)}, f32[4,32,2,128]{3,1,2,0:T(8,128)S(1)}, u32[]{:S(2)}, u32[]{:S(2)}) collective-permute-start(f32[4,32,2,128]{3,1,2,0:T(8,128)S(1)} %get-tuple-element.68), channel_id=1, source_target_pairs={{8,0},{16,8},{24,16},{9,1},{17,9},{25,17},{10,2},{18,10},{26,18},{... | collective-permute-start | bytes 393224 | tf_op jit(solution)/shard_map/ppermute | solution.py:30
  5.2 2.5 %collective-permute-start = (f32[4,32,2,128]{3,1,2,0:T(8,128)S(1)}, f32[4,32,2,128]{3,1,2,0:T(8,128)S(1)}, u32[]{:S(2)}, u32[]{:S(2)}) collective-permute-start(f32[4,32,2,128]{3,1,2,0:T(8,128)S(1)} %get-tuple-element.69), channel_id=1, source_target_pairs={{0,8},{8,16},{16,24},{1,9},{9,17},{17,25},{2,10},{10,18},{18,26},{... | collective-permute-start | bytes 393224 | tf_op jit(solution)/shard_map/ppermute | solution.py:29
  9.1 1.9 %collective-permute-start.8 = (bf16[10,32,2,128]{3,1,2,0:T(8,128)(2,1)S(1)}, bf16[10,32,2,128]{3,1,2,0:T(8,128)(2,1)S(1)}, u32[]{:S(2)}, u32[]{:S(2)}) collective-permute-start(bf16[10,32,2,128]{3,1,2,0:T(8,128)(2,1)S(1)} %copy.184), channel_id=1, source_target_pairs={{0,8},{8,16},{16,24},{1,9},{9,17},{17,25},{2,10},{10,18},{18,26},{... | collective-permute-start | bytes 491528 | tf_op jit(solution)/shard_map/ppermute | solution.py:29
  11.1 4.8 %collective-permute-start.9 = (bf16[10,32,2,128]{3,1,2,0:T(8,128)(2,1)S(1)}, bf16[10,32,2,128]{3,1,2,0:T(8,128)(2,1)S(1)}, u32[]{:S(2)}, u32[]{:S(2)}) collective-permute-start(bf16[10,32,2,128]{3,1,2,0:T(8,128)(2,1)S(1)} %copy.185), channel_id=1, source_target_pairs={{8,0},{16,8},{24,16},{9,1},{17,9},{25,17},{10,2},{18,10},{26,18},{... | collective-permute-start | bytes 491528 | tf_op jit(solution)/shard_map/ppermute | solution.py:30
  16.5 1.9 %collective-permute-start.2 = (f32[4,32,8,2]{3,1,2,0:T(8,128)S(1)}, f32[4,32,8,2]{3,1,2,0:T(8,128)S(1)}, u32[]{:S(2)}, u32[]{:S(2)}) collective-permute-start(f32[4,32,8,2]{3,1,2,0:T(8,128)S(1)} %get-tuple-element.51), channel_id=1, source_target_pairs={{1,0},{2,1},{3,2},{4,3},{5,4},{6,5},{7,6},{9,8},{10,9},{11,10},{12... | collective-permute-start | bytes 24584 | tf_op jit(solution)/shard_map/ppermute | solution.py:30
  18.5 2.4 %collective-permute-start.3 = (f32[4,32,8,2]{3,1,2,0:T(8,128)S(1)}, f32[4,32,8,2]{3,1,2,0:T(8,128)S(1)}, u32[]{:S(2)}, u32[]{:S(2)}) collective-permute-start(f32[4,32,8,2]{3,1,2,0:T(8,128)S(1)} %get-tuple-element.52), channel_id=1, source_target_pairs={{0,1},{1,2},{2,3},{3,4},{4,5},{5,6},{6,7},{8,9},{9,10},{10,11},{11... | collective-permute-start | bytes 24584 | tf_op jit(solution)/shard_map/ppermute | solution.py:29
  21.6 3.6 %collective-permute-done.2 = f32[4,32,8,2]{3,1,2,0:T(8,128)S(1)} collective-permute-done((f32[4,32,8,2]{3,1,2,0:T(8,128)S(1)}, f32[4,32,8,2]{3,1,2,0:T(8,128)S(1)}, u32[]{:S(2)}, u32[]{:S(2)}) %collective-permute-start.2) | collective-permute-done | bytes 8224 | tf_op jit(solution)/shard_map/ppermute | solution.py:30
  25.1 3.8 %collective-permute-done.3 = f32[4,32,8,2]{3,1,2,0:T(8,128)S(1)} collective-permute-done((f32[4,32,8,2]{3,1,2,0:T(8,128)S(1)}, f32[4,32,8,2]{3,1,2,0:T(8,128)S(1)}, u32[]{:S(2)}, u32[]{:S(2)}) %collective-permute-start.3) | collective-permute-done | bytes 8224 | tf_op jit(solution)/shard_map/ppermute | solution.py:29
  33.0 1.9 %collective-permute-start.11 = (bf16[10,32,8,2]{1,2,3,0:T(8,128)(2,1)S(1)}, bf16[10,32,8,2]{1,2,3,0:T(8,128)(2,1)S(1)}, u32[]{:S(2)}, u32[]{:S(2)}) collective-permute-start(bf16[10,32,8,2]{1,2,3,0:T(8,128)(2,1)S(1)} %copy.127), channel_id=1, source_target_pairs={{1,0},{2,1},{3,2},{4,3},{5,4},{6,5},{7,6},{9,8},{10,9},{11,10},{12... | collective-permute-start | bytes 30728 | tf_op jit(solution)/shard_map/ppermute | solution.py:30
  34.9 2.4 %collective-permute-start.10 = (bf16[10,32,8,2]{1,2,3,0:T(8,128)(2,1)S(1)}, bf16[10,32,8,2]{1,2,3,0:T(8,128)(2,1)S(1)}, u32[]{:S(2)}, u32[]{:S(2)}) collective-permute-start(bf16[10,32,8,2]{1,2,3,0:T(8,128)(2,1)S(1)} %copy.126), channel_id=1, source_target_pairs={{0,1},{1,2},{2,3},{3,4},{4,5},{5,6},{6,7},{8,9},{9,10},{10,11},{11... | collective-permute-start | bytes 30728 | tf_op jit(solution)/shard_map/ppermute | solution.py:29
  38.0 1.9 %collective-permute-start.4 = (f32[4,32,2,128]{3,1,2,0:T(8,128)}, f32[4,32,2,128]{3,1,2,0:T(8,128)S(1)}, u32[]{:S(2)}, u32[]{:S(2)}) collective-permute-start(f32[4,32,2,128]{3,1,2,0:T(8,128)} %get-tuple-element.61), channel_id=1, source_target_pairs={{0,8},{8,16},{16,24},{1,9},{9,17},{17,25},{2,10},{10,18},{18,26},{... | collective-permute-start | bytes 393224 | tf_op jit(solution)/shard_map/ppermute | solution.py:29
  39.9 4.8 %collective-permute-start.5 = (f32[4,32,2,128]{3,1,2,0:T(8,128)}, f32[4,32,2,128]{3,1,2,0:T(8,128)S(1)}, u32[]{:S(2)}, u32[]{:S(2)}) collective-permute-start(f32[4,32,2,128]{3,1,2,0:T(8,128)} %get-tuple-element.62), channel_id=1, source_target_pairs={{8,0},{16,8},{24,16},{9,1},{17,9},{25,17},{10,2},{18,10},{26,18},{... | collective-permute-start | bytes 393224 | tf_op jit(solution)/shard_map/ppermute | solution.py:30
  48.2 2.0 %multiply_add_fusion.1 = f32[10,32,4,129]{3,1,2,0:T(8,128)S(1)} fusion(f32[10,32,8,132]{3,1,2,0:T(8,128)S(1)} %maximum_convert_fusion, f32[32,4,129]{2,0,1:T(8,128)S(1)} %copy-done.3, f32[32,4,129]{2,0,1:T(8,128)S(1)} %get-tuple-element.21), kind=kLoop, calls=%fused_computation.7 | loop fusion | flops 3962880 | bytes 3434496 | tf_op jit(solution)/shard_map/add | solution.py:73
  50.4 1.9 %collective-permute-start.12 = (bf16[10,32,2,128]{3,1,2,0:T(8,128)(2,1)S(1)}, bf16[10,32,2,128]{3,1,2,0:T(8,128)(2,1)S(1)}, u32[]{:S(2)}, u32[]{:S(2)}) collective-permute-start(bf16[10,32,2,128]{3,1,2,0:T(8,128)(2,1)S(1)} %get-tuple-element.53), channel_id=1, source_target_pairs={{0,8},{8,16},{16,24},{1,9},{9,17},{17,25},{2,10},{10,18},{18,26},{... | collective-permute-start | bytes 491528 | tf_op jit(solution)/shard_map/ppermute | solution.py:29
  52.4 4.8 %collective-permute-start.13 = (bf16[10,32,2,128]{3,1,2,0:T(8,128)(2,1)S(1)}, bf16[10,32,2,128]{3,1,2,0:T(8,128)(2,1)S(1)}, u32[]{:S(2)}, u32[]{:S(2)}) collective-permute-start(bf16[10,32,2,128]{3,1,2,0:T(8,128)(2,1)S(1)} %get-tuple-element.54), channel_id=1, source_target_pairs={{8,0},{16,8},{24,16},{9,1},{17,9},{25,17},{10,2},{18,10},{26,18},{... | collective-permute-start | bytes 491528 | tf_op jit(solution)/shard_map/ppermute | solution.py:30
  57.5 2.0 %collective-permute-start.6 = (f32[4,32,8,2]{3,1,2,0:T(8,128)S(1)}, f32[4,32,8,2]{3,1,2,0:T(8,128)S(1)}, u32[]{:S(2)}, u32[]{:S(2)}) collective-permute-start(f32[4,32,8,2]{3,1,2,0:T(8,128)S(1)} %get-tuple-element.47), channel_id=1, source_target_pairs={{1,0},{2,1},{3,2},{4,3},{5,4},{6,5},{7,6},{9,8},{10,9},{11,10},{12... | collective-permute-start | bytes 24584 | tf_op jit(solution)/shard_map/ppermute | solution.py:30
  59.5 2.3 %collective-permute-start.7 = (f32[4,32,8,2]{3,1,2,0:T(8,128)S(1)}, f32[4,32,8,2]{3,1,2,0:T(8,128)S(1)}, u32[]{:S(2)}, u32[]{:S(2)}) collective-permute-start(f32[4,32,8,2]{3,1,2,0:T(8,128)S(1)} %get-tuple-element.48), channel_id=1, source_target_pairs={{0,1},{1,2},{2,3},{3,4},{4,5},{5,6},{6,7},{8,9},{9,10},{10,11},{11... | collective-permute-start | bytes 24584 | tf_op jit(solution)/shard_map/ppermute | solution.py:29
  62.5 3.7 %collective-permute-done.6 = f32[4,32,8,2]{3,1,2,0:T(8,128)S(1)} collective-permute-done((f32[4,32,8,2]{3,1,2,0:T(8,128)S(1)}, f32[4,32,8,2]{3,1,2,0:T(8,128)S(1)}, u32[]{:S(2)}, u32[]{:S(2)}) %collective-permute-start.6) | collective-permute-done | bytes 8224 | tf_op jit(solution)/shard_map/ppermute | solution.py:30
  66.2 3.8 %collective-permute-done.7 = f32[4,32,8,2]{3,1,2,0:T(8,128)S(1)} collective-permute-done((f32[4,32,8,2]{3,1,2,0:T(8,128)S(1)}, f32[4,32,8,2]{3,1,2,0:T(8,128)S(1)}, u32[]{:S(2)}, u32[]{:S(2)}) %collective-permute-start.7) | collective-permute-done | bytes 8224 | tf_op jit(solution)/shard_map/ppermute | solution.py:29
  72.4 1.9 %collective-permute-start.15 = (bf16[10,32,8,2]{1,2,3,0:T(8,128)(2,1)S(1)}, bf16[10,32,8,2]{1,2,3,0:T(8,128)(2,1)S(1)}, u32[]{:S(2)}, u32[]{:S(2)}) collective-permute-start(bf16[10,32,8,2]{1,2,3,0:T(8,128)(2,1)S(1)} %copy.131), channel_id=1, source_target_pairs={{1,0},{2,1},{3,2},{4,3},{5,4},{6,5},{7,6},{9,8},{10,9},{11,10},{12... | collective-permute-start | bytes 30728 | tf_op jit(solution)/shard_map/ppermute | solution.py:30
  74.4 2.6 %collective-permute-start.14 = (bf16[10,32,8,2]{1,2,3,0:T(8,128)(2,1)S(1)}, bf16[10,32,8,2]{1,2,3,0:T(8,128)(2,1)S(1)}, u32[]{:S(2)}, u32[]{:S(2)}) collective-permute-start(bf16[10,32,8,2]{1,2,3,0:T(8,128)(2,1)S(1)} %copy.130), channel_id=1, source_target_pairs={{0,1},{1,2},{2,3},{3,4},{4,5},{5,6},{6,7},{8,9},{9,10},{10,11},{11... | collective-permute-start | bytes 30728 | tf_op jit(solution)/shard_map/ppermute | solution.py:29
  77.0 2.7 %collective-permute-done.14 = bf16[10,32,8,2]{1,2,3,0:T(8,128)(2,1)S(1)} collective-permute-done((bf16[10,32,8,2]{1,2,3,0:T(8,128)(2,1)S(1)}, bf16[10,32,8,2]{1,2,3,0:T(8,128)(2,1)S(1)}, u32[]{:S(2)}, u32[]{:S(2)}) %collective-permute-start.14) | collective-permute-done | bytes 10272 | tf_op jit(solution)/shard_map/ppermute | solution.py:29
  83.1 2.0 %multiply_add_fusion = f32[10,32,4,129]{3,1,2,0:T(8,128)S(1)} fusion(f32[10,32,8,132]{3,1,2,0:T(8,128)S(1)} %maximum_convert_fusion.1, f32[32,4,129]{2,0,1:T(8,128)S(1)} %minimum_bitcast_fusion, f32[32,4,129]{2,0,1:T(8,128)S(1)} %get-tuple-element.17), kind=kLoop, calls=%fused_computation.6 | loop fusion | flops 3962880 | bytes 3434496 | tf_op jit(solution)/shard_map/add | solution.py:73
  85.4 1.5 %fusion = f32[32,4,128,10]{2,3,1,0:T(8,128)S(1)} fusion(f32[10,32,4,128]{3,1,2,0:T(8,128)S(1)} %fusion.4, f32[10,10]{1,0:T(8,128)S(1)} %copy-done), kind=kOutput, calls=%fused_computation.8 | convolution fusion | flops 19660800 | bytes 1311120 | tf_op jit(solution)/shard_map/ab,bzyx->azyx/dot_general | solution.py:108
  (105 shorter events, 22.0 us)
Async XLA Ops:
  0.6 84.8 %copy-start = (f32[10,10]{1,0:T(8,128)S(1)}, f32[10,10]{1,0:T(8,128)}, u32[]{:S(2)}) copy-start(f32[10,10]{1,0:T(8,128)} %param.9) | copy-start | bytes 1204
  0.6 15.3 %copy-start.10 = (s32[1,8]{1,0:T(1,128)S(1)}, s32[1,8]{1,0:T(1,128)}, u32[]{:S(2)}) copy-start(s32[1,8]{1,0:T(1,128)} %param.7) | copy-start | bytes 100
  0.7 15.5 %copy-start.9 = (f32[4,128]{1,0:T(4,128)S(1)}, f32[4,128]{1,0:T(4,128)}, u32[]{:S(2)}) copy-start(f32[4,128]{1,0:T(4,128)} %param.8) | copy-start | bytes 6148
  1.7 14.5 %copy-start.1 = (f32[4,32,4,128]{3,2,1,0:T(4,128)S(1)}, f32[4,32,4,128]{3,2,1,0:T(4,128)}, u32[]{:S(2)}) copy-start(f32[4,32,4,128]{3,2,1,0:T(4,128)} %param.5) | copy-start | bytes 786436
  1.7 14.6 %collective-permute-start.1 = (f32[4,32,2,128]{3,1,2,0:T(8,128)S(1)}, f32[4,32,2,128]{3,1,2,0:T(8,128)S(1)}, u32[]{:S(2)}, u32[]{:S(2)}) collective-permute-start(f32[4,32,2,128]{3,1,2,0:T(8,128)S(1)} %get-tuple-element.68), channel_id=1, source_target_pairs={{8,0},{16,8},{24,16},{9,1},{17,9},{25,17},{10,2},{18,10},{26,18},{... | collective-permute-start | bytes 393224 | tf_op jit(solution)/shard_map/ppermute | solution.py:30
  5.2 11.0 %collective-permute-start = (f32[4,32,2,128]{3,1,2,0:T(8,128)S(1)}, f32[4,32,2,128]{3,1,2,0:T(8,128)S(1)}, u32[]{:S(2)}, u32[]{:S(2)}) collective-permute-start(f32[4,32,2,128]{3,1,2,0:T(8,128)S(1)} %get-tuple-element.69), channel_id=1, source_target_pairs={{0,8},{8,16},{16,24},{1,9},{9,17},{17,25},{2,10},{10,18},{18,26},{... | collective-permute-start | bytes 393224 | tf_op jit(solution)/shard_map/ppermute | solution.py:29
  9.1 22.1 %collective-permute-start.8 = (bf16[10,32,2,128]{3,1,2,0:T(8,128)(2,1)S(1)}, bf16[10,32,2,128]{3,1,2,0:T(8,128)(2,1)S(1)}, u32[]{:S(2)}, u32[]{:S(2)}) collective-permute-start(bf16[10,32,2,128]{3,1,2,0:T(8,128)(2,1)S(1)} %copy.184), channel_id=1, source_target_pairs={{0,8},{8,16},{16,24},{1,9},{9,17},{17,25},{2,10},{10,18},{18,26},{... | collective-permute-start | bytes 491528 | tf_op jit(solution)/shard_map/ppermute | solution.py:29
  11.1 20.4 %collective-permute-start.9 = (bf16[10,32,2,128]{3,1,2,0:T(8,128)(2,1)S(1)}, bf16[10,32,2,128]{3,1,2,0:T(8,128)(2,1)S(1)}, u32[]{:S(2)}, u32[]{:S(2)}) collective-permute-start(bf16[10,32,2,128]{3,1,2,0:T(8,128)(2,1)S(1)} %copy.185), channel_id=1, source_target_pairs={{8,0},{16,8},{24,16},{9,1},{17,9},{25,17},{10,2},{18,10},{26,18},{... | collective-permute-start | bytes 491528 | tf_op jit(solution)/shard_map/ppermute | solution.py:30
  16.5 8.6 %collective-permute-start.2 = (f32[4,32,8,2]{3,1,2,0:T(8,128)S(1)}, f32[4,32,8,2]{3,1,2,0:T(8,128)S(1)}, u32[]{:S(2)}, u32[]{:S(2)}) collective-permute-start(f32[4,32,8,2]{3,1,2,0:T(8,128)S(1)} %get-tuple-element.51), channel_id=1, source_target_pairs={{1,0},{2,1},{3,2},{4,3},{5,4},{6,5},{7,6},{9,8},{10,9},{11,10},{12... | collective-permute-start | bytes 24584 | tf_op jit(solution)/shard_map/ppermute | solution.py:30
  18.5 10.5 %collective-permute-start.3 = (f32[4,32,8,2]{3,1,2,0:T(8,128)S(1)}, f32[4,32,8,2]{3,1,2,0:T(8,128)S(1)}, u32[]{:S(2)}, u32[]{:S(2)}) collective-permute-start(f32[4,32,8,2]{3,1,2,0:T(8,128)S(1)} %get-tuple-element.52), channel_id=1, source_target_pairs={{0,1},{1,2},{2,3},{3,4},{4,5},{5,6},{6,7},{8,9},{9,10},{10,11},{11... | collective-permute-start | bytes 24584 | tf_op jit(solution)/shard_map/ppermute | solution.py:29
  30.5 1.0 %copy-start.2 = (bf16[10,32,4,128]{3,2,1,0:T(4,128)(2,1)S(1)}, bf16[10,32,4,128]{3,2,1,0:T(4,128)(2,1)}, u32[]{:S(2)}) copy-start(bf16[10,32,4,128]{3,2,1,0:T(4,128)(2,1)} %param.6) | copy-start | bytes 983044
  33.0 12.4 %collective-permute-start.11 = (bf16[10,32,8,2]{1,2,3,0:T(8,128)(2,1)S(1)}, bf16[10,32,8,2]{1,2,3,0:T(8,128)(2,1)S(1)}, u32[]{:S(2)}, u32[]{:S(2)}) collective-permute-start(bf16[10,32,8,2]{1,2,3,0:T(8,128)(2,1)S(1)} %copy.127), channel_id=1, source_target_pairs={{1,0},{2,1},{3,2},{4,3},{5,4},{6,5},{7,6},{9,8},{10,9},{11,10},{12... | collective-permute-start | bytes 30728 | tf_op jit(solution)/shard_map/ppermute | solution.py:30
  34.9 9.8 %collective-permute-start.10 = (bf16[10,32,8,2]{1,2,3,0:T(8,128)(2,1)S(1)}, bf16[10,32,8,2]{1,2,3,0:T(8,128)(2,1)S(1)}, u32[]{:S(2)}, u32[]{:S(2)}) collective-permute-start(bf16[10,32,8,2]{1,2,3,0:T(8,128)(2,1)S(1)} %copy.126), channel_id=1, source_target_pairs={{0,1},{1,2},{2,3},{3,4},{4,5},{5,6},{6,7},{8,9},{9,10},{10,11},{11... | collective-permute-start | bytes 30728 | tf_op jit(solution)/shard_map/ppermute | solution.py:29
  38.0 19.2 %collective-permute-start.4 = (f32[4,32,2,128]{3,1,2,0:T(8,128)}, f32[4,32,2,128]{3,1,2,0:T(8,128)S(1)}, u32[]{:S(2)}, u32[]{:S(2)}) collective-permute-start(f32[4,32,2,128]{3,1,2,0:T(8,128)} %get-tuple-element.61), channel_id=1, source_target_pairs={{0,8},{8,16},{16,24},{1,9},{9,17},{17,25},{2,10},{10,18},{18,26},{... | collective-permute-start | bytes 393224 | tf_op jit(solution)/shard_map/ppermute | solution.py:29
  39.9 17.3 %collective-permute-start.5 = (f32[4,32,2,128]{3,1,2,0:T(8,128)}, f32[4,32,2,128]{3,1,2,0:T(8,128)S(1)}, u32[]{:S(2)}, u32[]{:S(2)}) collective-permute-start(f32[4,32,2,128]{3,1,2,0:T(8,128)} %get-tuple-element.62), channel_id=1, source_target_pairs={{8,0},{16,8},{24,16},{9,1},{17,9},{25,17},{10,2},{18,10},{26,18},{... | collective-permute-start | bytes 393224 | tf_op jit(solution)/shard_map/ppermute | solution.py:30
  46.9 1.3 %copy-start.3 = (f32[32,4,129]{2,0,1:T(8,128)S(1)}, f32[32,4,129]{2,0,1:T(8,128)}, u32[]{:S(2)}) copy-start(f32[32,4,129]{2,0,1:T(8,128)} %minimum_bitcast_fusion.1) | copy-start | bytes 198148
  50.4 20.5 %collective-permute-start.12 = (bf16[10,32,2,128]{3,1,2,0:T(8,128)(2,1)S(1)}, bf16[10,32,2,128]{3,1,2,0:T(8,128)(2,1)S(1)}, u32[]{:S(2)}, u32[]{:S(2)}) collective-permute-start(bf16[10,32,2,128]{3,1,2,0:T(8,128)(2,1)S(1)} %get-tuple-element.53), channel_id=1, source_target_pairs={{0,8},{8,16},{16,24},{1,9},{9,17},{17,25},{2,10},{10,18},{18,26},{... | collective-permute-start | bytes 491528 | tf_op jit(solution)/shard_map/ppermute | solution.py:29
  52.4 18.6 %collective-permute-start.13 = (bf16[10,32,2,128]{3,1,2,0:T(8,128)(2,1)S(1)}, bf16[10,32,2,128]{3,1,2,0:T(8,128)(2,1)S(1)}, u32[]{:S(2)}, u32[]{:S(2)}) collective-permute-start(bf16[10,32,2,128]{3,1,2,0:T(8,128)(2,1)S(1)} %get-tuple-element.54), channel_id=1, source_target_pairs={{8,0},{16,8},{24,16},{9,1},{17,9},{25,17},{10,2},{18,10},{26,18},{... | collective-permute-start | bytes 491528 | tf_op jit(solution)/shard_map/ppermute | solution.py:30
  57.5 8.7 %collective-permute-start.6 = (f32[4,32,8,2]{3,1,2,0:T(8,128)S(1)}, f32[4,32,8,2]{3,1,2,0:T(8,128)S(1)}, u32[]{:S(2)}, u32[]{:S(2)}) collective-permute-start(f32[4,32,8,2]{3,1,2,0:T(8,128)S(1)} %get-tuple-element.47), channel_id=1, source_target_pairs={{1,0},{2,1},{3,2},{4,3},{5,4},{6,5},{7,6},{9,8},{10,9},{11,10},{12... | collective-permute-start | bytes 24584 | tf_op jit(solution)/shard_map/ppermute | solution.py:30
  59.5 10.5 %collective-permute-start.7 = (f32[4,32,8,2]{3,1,2,0:T(8,128)S(1)}, f32[4,32,8,2]{3,1,2,0:T(8,128)S(1)}, u32[]{:S(2)}, u32[]{:S(2)}) collective-permute-start(f32[4,32,8,2]{3,1,2,0:T(8,128)S(1)} %get-tuple-element.48), channel_id=1, source_target_pairs={{0,1},{1,2},{2,3},{3,4},{4,5},{5,6},{6,7},{8,9},{9,10},{10,11},{11... | collective-permute-start | bytes 24584 | tf_op jit(solution)/shard_map/ppermute | solution.py:29
  62.5 8.0 %copy-start.7 = (f32[32,4,128]{2,0,1:T(8,128)S(1)}, f32[32,4,128]{2,0,1:T(8,128)}, u32[]{:S(2)}) copy-start(f32[32,4,128]{2,0,1:T(8,128)} %get-tuple-element.59) | copy-start | bytes 196612
  62.5 8.0 %copy-start.8 = (f32[32,4,128]{2,0,1:T(8,128)S(1)}, f32[32,4,128]{2,0,1:T(8,128)}, u32[]{:S(2)}) copy-start(f32[32,4,128]{2,0,1:T(8,128)} %get-tuple-element.60) | copy-start | bytes 196612
  72.4 7.8 %collective-permute-start.15 = (bf16[10,32,8,2]{1,2,3,0:T(8,128)(2,1)S(1)}, bf16[10,32,8,2]{1,2,3,0:T(8,128)(2,1)S(1)}, u32[]{:S(2)}, u32[]{:S(2)}) collective-permute-start(bf16[10,32,8,2]{1,2,3,0:T(8,128)(2,1)S(1)} %copy.131), channel_id=1, source_target_pairs={{1,0},{2,1},{3,2},{4,3},{5,4},{6,5},{7,6},{9,8},{10,9},{11,10},{12... | collective-permute-start | bytes 30728 | tf_op jit(solution)/shard_map/ppermute | solution.py:30
  74.4 5.3 %collective-permute-start.14 = (bf16[10,32,8,2]{1,2,3,0:T(8,128)(2,1)S(1)}, bf16[10,32,8,2]{1,2,3,0:T(8,128)(2,1)S(1)}, u32[]{:S(2)}, u32[]{:S(2)}) collective-permute-start(bf16[10,32,8,2]{1,2,3,0:T(8,128)(2,1)S(1)} %copy.130), channel_id=1, source_target_pairs={{0,1},{1,2},{2,3},{3,4},{4,5},{5,6},{6,7},{8,9},{9,10},{10,11},{11... | collective-permute-start | bytes 30728 | tf_op jit(solution)/shard_map/ppermute | solution.py:29
  (3 other events, 2.7 us)
where the time goes:
time: 90.7 us; the launch traced here: 90 us
  starting transfers between devices  43.7 us (48%)
  waiting for transfers between devices  17.6 us (19%)
  other arithmetic  13.7 us (15%)
  local copies, waits for them, and re-layouts  12.2 us (13%)
  matrix products  1.54 us (2%)
  between operations  1.32 us (1%)
    ppermute x8, starting transfers between devices, extended(): after = lax.ppermute(first, axis, down)  25.7 us
    ppermute x8, starting transfers between devices, extended(): before = lax.ppermute(last, axis, up)  17.9 us
    ppermute x8, waiting for transfers between devices, extended(): before = lax.ppermute(last, axis, up)  10.3 us
    ppermute x8, waiting for transfers between devices, extended(): after = lax.ppermute(first, axis, down)  7.28 us
    add x4, other arithmetic, limited_divergence(): jnp.maximum(face_speed, 0.0) * left_value  6.47 us
    unnamed x32, local copies, waits for them, and re-layouts  4.23 us
    slice x6, local copies, waits for them, and re-layouts, extended(): first = lax.slice_in_dim(array, 0, width, axis=dim)  2.99 us
    slice x6, local copies, waits for them, and re-layouts, extended(): last = lax.slice_in_dim(array, length - width, length, axis=dim)  2.38 us
  transfers between devices with their start and end apart: 16, of which 5 were waited for; matrix products, arithmetic and copies ran while one was open for 15% of the time, Pallas kernels for 0%

commit v1 on v0

v1 whole, which is shorter than its diff:
```python
import functools

import jax
import jax.numpy as jnp
from jax import lax
from jax.experimental import pallas as pl
from jax.experimental.pallas import tpu as pltpu
from jax.sharding import PartitionSpec as P

WBY = 4
WBX = 16

time_step = 0.3
coriolis = 0.2
viscosity = 0.1
diffusion = 0.05
thermal = 0.2
haline = 0.15
gravity_red = 0.05
react_step = 0.5
water_atten = 0.3
chloro_atten = 0.2

MESH = pl.DeviceIdType.MESH
F32 = jnp.float32
BF16 = jnp.bfloat16
GROUP = 8
HALO = 4
RIM = [(0, 1), (0, 2), (1, 1), (1, 2), (1, 3), (2, 1), (2, 2), (3, 1), (3, 2)]
DIRS = [(dy, dx) for dy in (-1, 0, 1) for dx in (-1, 0, 1) if (dy, dx) != (0, 0)]


def minmod(a, b):
    return jnp.maximum(jnp.minimum(a, b), 0.0) + jnp.minimum(jnp.maximum(a, b), 0.0)


def lanes(x, shift):
    return pltpu.roll(x, shift % x.shape[1], 1)


def lane_of(shape):
    return lax.broadcasted_iota(jnp.int32, shape, 1)


def depth_sum(x):
    level = lax.broadcasted_iota(jnp.int32, x.shape, 0)
    step = 1
    while step < x.shape[0]:
        x = x + jnp.where(level >= step, pltpu.roll(x, step, 0), 0.0)
        step *= 2
    return x


def over_groups(x):
    step = GROUP
    while step < x.shape[1]:
        x = x + lanes(x, step)
        step *= 2
    return x


def split_speed(speed):
    return jnp.maximum(speed, 0.0), jnp.minimum(speed, 0.0)


def kernel(ngrp, ntile, tr, oc, wet, light, rates, oc_out, tr_out, heat_out,
           halo_tr, halo_oc, send_oc, px, st, oe, o1, m1, z1, m2, z2, ua, va, ub, vb, tt,
           p_send, p_recv, o_send, o_recv, t_send, t_recv):
    ntr, ny, nz, nx = tr.shape
    gy, gx = lax.axis_index("grp"), lax.axis_index("tile")
    there = {-1: gy > 0, 0: True, 1: gy < ngrp - 1}
    over = {-1: gx > 0, 0: True, 1: gx < ntile - 1}

    def has(dy, dx):
        return jnp.logical_and(there[dy], over[dx])

    def peer(dy, dx):
        return (gy + dy, gx + dx)

    barrier = pltpu.get_barrier_semaphore()
    for dy, dx in DIRS:
        @pl.when(has(dy, dx))
        def _(dy=dy, dx=dx):
            pl.semaphore_signal(barrier, inc=1, device_id=peer(dy, dx), device_id_type=MESH)

    num_y = 1 + there[-1].astype(jnp.int32) + there[1].astype(jnp.int32)
    num_x = 1 + over[-1].astype(jnp.int32) + over[1].astype(jnp.int32)

    for slot, (field, depth) in enumerate(RIM):
        send_oc[1, slot] = oc[field, ny - depth].astype(BF16)
        send_oc[0, slot] = oc[field, depth - 1].astype(BF16)

    lane = lane_of((nz, nx))

    def pack(row, carry):
        total = jnp.zeros((nz, nx), F32)
        for field in range(ntr + 4):
            x = tr[field, row].astype(F32) if field < ntr else oc[field - ntr, row]
            total = jnp.where(lane // GROUP == field, lanes(x, GROUP * field + GROUP // 2), total)
        px[1, row + 2] = total.astype(BF16)
        return carry

    lax.fori_loop(0, ny, pack, 0)

    def edge_copy(dy, dx, index):
        rows = {-1: (2, ny + 2, 2), 0: (2, 2, ny), 1: (ny, 0, 2)}[dy]
        return pltpu.make_async_remote_copy(
            src_ref=px.at[1, pl.ds(rows[0], rows[2])], dst_ref=px.at[1 - dx, pl.ds(rows[1], rows[2])],
            send_sem=p_send.at[index], recv_sem=p_recv.at[index], device_id=peer(dy, dx), device_id_type=MESH)

    def ocean_copy(side):
        return pltpu.make_async_remote_copy(
            src_ref=send_oc.at[side], dst_ref=halo_oc.at[side],
            send_sem=o_send.at[side], recv_sem=o_recv.at[side],
            device_id=peer(2 * side - 1, 0), device_id_type=MESH)

    def tracer_copy(side, t):
        return pltpu.make_async_remote_copy(
            src_ref=tr.at[t, pl.ds(side * (ny - HALO), HALO)], dst_ref=halo_tr.at[side, t],
            send_sem=t_send.at[side, t], recv_sem=t_recv.at[side, t],
            device_id=peer(2 * side - 1, 0), device_id_type=MESH)

    pl.semaphore_wait(barrier, num_y * num_x - 1)
    for index, (dy, dx) in enumerate(DIRS):
        @pl.when(has(dy, dx))
        def _(dy=dy, dx=dx, index=index):
            edge_copy(dy, dx, index).start()
    for side in (0, 1):
        @pl.when(there[2 * side - 1])
        def _(side=side):
            ocean_copy(side).start()
    for t in range(ntr):
        for side in (0, 1):
            @pl.when(there[2 * side - 1])
            def _(side=side, t=t):
                tracer_copy(side, t).start()

    for index, (dy, dx) in enumerate(DIRS):
        @pl.when(jnp.logical_not(has(-dy, -dx)))
        def _(dy=dy, dx=dx):
            start, size = {-1: (ny + 2, 2), 0: (2, ny), 1: (0, 2)}[dy]
            px[1 - dx, pl.ds(start, size)] = jnp.zeros((size, nz, nx), BF16)
    for side in (0, 1):
        @pl.when(jnp.logical_not(there[1 - 2 * side]))
        def _(side=side):
            halo_oc[side] = jnp.zeros(halo_oc.shape[1:], BF16)
            halo_tr[side] = jnp.zeros(halo_tr.shape[1:], BF16)

    for field in range(4):
        for row in range(ny):
            oe[field, row + 3] = oc[field, row]

    for index, (dy, dx) in enumerate(DIRS):
        @pl.when(has(-dy, -dx))
        def _(dy=dy, dx=dx, index=index):
            edge_copy(dy, dx, index).wait_recv()

    part = lane % GROUP
    near_west = part == GROUP // 2

    def strips(slot, carry):
        west, own, east = (px[k, slot].astype(F32) for k in range(3))
        low = part < GROUP // 2
        left = jnp.where(low, west, own)
        right = jnp.where(low, own, east)
        st[0, slot], st[1, slot] = left, right
        mid = jnp.where(near_west, lanes(left, 1), lanes(right, -1))
        far = jnp.where(near_west, lanes(left, 2), lanes(right, -2))
        close = jnp.where(near_west, left, right)
        m1[slot] = mid
        z1[slot] = mid + 0.5 * minmod(mid - far, close - mid)
        return carry

    lax.fori_loop(0, ny + 4, strips, 0)

    group = lane // GROUP
    buoyancy = jnp.where(group == ntr + 2, thermal, 0.0) - jnp.where(group == ntr + 3, haline, 0.0)
    blend = jnp.where(group < ntr + 2, viscosity, diffusion)

    def strip_step(side, slot):
        c = [st[side, slot + k] for k in (-2, -1, 0, 1, 2)]
        mid = c[2]
        zonal = over_groups(jnp.where(group == ntr, mid, 0.0))
        merid = [over_groups(jnp.where(group == ntr + 1, x, 0.0)) for x in c[1:4]]
        east, west, north, south = lanes(mid, -1), lanes(mid, 1), c[3], c[1]
        gx_, gy_ = 0.5 * (east - west), 0.5 * (north - south)
        lap = east + west + north + south - 4.0 * mid
        px_ = gravity_red * depth_sum(over_groups(buoyancy * gx_))
        py_ = gravity_red * depth_sum(over_groups(buoyancy * gy_))
        rate = blend * lap - (zonal * gx_ + merid[1] * gy_)
        rate = rate + jnp.where(group == ntr, coriolis * merid[1] - px_, 0.0)
        rate = rate - jnp.where(group == ntr + 1, coriolis * zonal + py_, 0.0)
        ocean_one = mid + time_step * rate
        diff = mid - west
        half = 0.5 * minmod(diff, lanes(diff, -1))
        plus, minus = split_speed(0.5 * (zonal + lanes(zonal, 1)))
        flux = plus * lanes(mid + half, 1) + minus * (mid - half)
        div = lanes(flux, -1) - flux
        d = [c[k + 1] - c[k] for k in range(4)]
        h = [0.5 * minmod(d[k], d[k + 1]) for k in range(3)]
        fluxes = []
        for k in (0, 1):
            plus, minus = split_speed(0.5 * (merid[k] + merid[k + 1]))
            fluxes.append(plus * (c[k + 1] + h[k]) + minus * (c[k + 2] - h[k + 1]))
        div = div + (fluxes[1] - fluxes[0])
        tracer_one = (mid - time_step * div).astype(BF16).astype(F32)
        return jnp.where(group < ntr, tracer_one, ocean_one)

    in_west = jnp.where(over[-1], 1.0, 0.0)
    in_east = jnp.where(over[1], 1.0, 0.0)

    def strip_row(row, carry):
        left = strip_step(0, row + 2)
        right = strip_step(1, row + 2)
        mid = jnp.where(near_west, in_west * lanes(left, 1), in_east * lanes(right, -1))
        far = jnp.where(near_west, in_west * lanes(left, 2), in_east * lanes(right, -2))
        close = jnp.where(near_west, left, right)
        m2[row] = mid
        z2[row] = mid + 0.5 * minmod(mid - far, close - mid)
        return carry

    lax.fori_loop(0, ny, strip_row, 0)

    for side in (0, 1):
        @pl.when(there[1 - 2 * side])
        def _(side=side):
            ocean_copy(side).wait_recv()
    for slot, (field, depth) in enumerate(RIM):
        oe[field, 3 - depth] = halo_oc[1, slot].astype(F32)
        oe[field, ny + 2 + depth] = halo_oc[0, slot].astype(F32)

    first, last = lane == 0, lane == nx - 1

    def shift_back(field):
        return -(GROUP * field + GROUP // 2)

    def ocean_rates(get, edge):
        center = [get(f, 0) for f in range(4)]
        zonal, merid = center[0], center[1]
        rates_, grads = [], []
        for f in range(4):
            mid = center[f]
            rim = lanes(edge, shift_back(ntr + f))
            east = jnp.where(last, rim, lanes(mid, -1))
            west = jnp.where(first, rim, lanes(mid, 1))
            north, south = get(f, 1), get(f, -1)
            gx_, gy_ = 0.5 * (east - west), 0.5 * (north - south)
            lap = east + west + north + south - 4.0 * mid
            rates_.append((viscosity if f < 2 else diffusion) * lap - (zonal * gx_ + merid * gy_))
            grads.append((gx_, gy_))
        px_, py_ = (gravity_red * depth_sum(thermal * grads[2][k] - haline * grads[3][k]) for k in (0, 1))
        rates_[0] = rates_[0] + coriolis * merid - px_
        rates_[1] = rates_[1] - coriolis * zonal - py_
        return rates_

    in_south = jnp.where(there[-1], 1.0, 0.0)
    in_north = jnp.where(there[1], 1.0, 0.0)

    def ocean_first(k, carry):
        keep = jnp.where(k == 0, in_south, jnp.where(k == ny + 1, in_north, 1.0))
        rate = ocean_rates(lambda f, dy: oe[f, k + 2 + dy], m1[k + 1])
        for f in range(4):
            o1[f, k] = keep * (oe[f, k + 2] + time_step * rate[f])
        return carry

    lax.fori_loop(0, ny + 2, ocean_first, 0)

    def ocean_second(row, carry):
        rate = ocean_rates(lambda f, dy: o1[f, row + 1 + dy], m2[row])
        for f in range(4):
            oc_out[f, row] = 0.5 * (oe[f, row + 3] + o1[f, row + 1] + time_step * rate[f])
        return carry

    lax.fori_loop(0, ny, ocean_second, 0)

    def zonal_faces(scale, mid, edge):
        rim = lanes(edge, shift_back(ntr))
        east = jnp.where(last, rim, lanes(mid, -1))
        west = jnp.where(first, rim, lanes(mid, 1))
        return split_speed(scale * (west + mid)) + split_speed(scale * (mid + east))

    def faces_first(j, carry):
        for k, x in enumerate(zonal_faces(0.5 * time_step, oe[0, j + 1], m1[j])):
            ua[k, j] = x
        return carry

    lax.fori_loop(0, ny + 4, faces_first, 0)

    def faces_second(j, carry):
        for k, x in enumerate(zonal_faces(0.25 * time_step, o1[0, j + 1], m2[j])):
            ub[k, j] = x
        return carry

    lax.fori_loop(0, ny, faces_second, 0)

    def merid_first(j, carry):
        va[0, j], va[1, j] = split_speed((0.5 * time_step) * (oe[1, j] + oe[1, j + 1]))
        return carry

    lax.fori_loop(0, ny + 5, merid_first, 0)

    def merid_second(j, carry):
        vb[0, j], vb[1, j] = split_speed((0.25 * time_step) * (o1[1, j] + o1[1, j + 1]))
        return carry

    lax.fori_loop(0, ny + 1, merid_second, 0)

    chunk = 16
    clane = lane_of((chunk, nx))
    cfirst, clast = clane == 0, clane == nx - 1

    def zonal_part(c, rim, rim_value, speeds):
        diff = c - jnp.where(cfirst, rim, lanes(c, 1))
        ahead = jnp.where(clast, rim - c, lanes(diff, -1))
        half = 0.5 * minmod(diff, ahead)
        left, right = c + half, c - half
        before = jnp.where(cfirst, rim_value, lanes(left, 1))
        after = jnp.where(clast, rim_value, lanes(right, -1))
        return (speeds[2] * left + speeds[3] * after) - (speeds[0] * before + speeds[1] * right)

    def merid_part(c, speeds):
        d = [b - a for a, b in zip(c[:-1], c[1:])]
        h = [0.5 * minmod(a, b) for a, b in zip(d[:-1], d[1:])]
        flux = []
        for k in range(len(h) - 1):
            plus, minus = speeds(k)
            flux.append(plus * (c[k + 1] + h[k]) + minus * (c[k + 2] - h[k + 1]))
        return [b - a for a, b in zip(flux[:-1], flux[1:])]

    def tracer(t, carry):
        for side in (0, 1):
            @pl.when(there[1 - 2 * side])
            def _(side=side):
                tracer_copy(side, t).wait_recv()
        back = nx - (GROUP * t + GROUP // 2)

        def levels(zc, inner):
            zs = pl.ds(pl.multiple_of(zc * chunk, chunk), chunk)
            c = [halo_tr[1, t, k, zs].astype(F32) for k in range(HALO)]
            c += [tr[t, k, zs].astype(F32) for k in range(ny)]
            c += [halo_tr[0, t, k, zs].astype(F32) for k in range(HALO)]
            along_y = merid_part(c, lambda k: (va[0, k, zs], va[1, k, zs]))
            one = []
            for j in range(ny + 4):
                rim = pltpu.roll(m1[j, zs], back, 1)
                rim_value = pltpu.roll(z1[j, zs], back, 1)
                mid = c[j + 2]
                div = zonal_part(mid, rim, rim_value, [ua[k, j, zs] for k in range(4)]) + along_y[j]
                new = (mid - div).astype(BF16).astype(F32)
                if j < 2:
                    new = in_south * new
                if j >= ny + 2:
                    new = in_north * new
                one.append(new)
            along_y = merid_part(one, lambda k: (vb[0, k, zs], vb[1, k, zs]))
            for j in range(ny):
                rim = pltpu.roll(m2[j, zs], back, 1)
                rim_value = pltpu.roll(z2[j, zs], back, 1)
                mid = one[j + 2]
                div = zonal_part(mid, rim, rim_value, [ub[k, j, zs] for k in range(4)]) + along_y[j]
                tt[t, j, zs] = 0.5 * (c[j + 4] + mid) - div
            return inner

        lax.fori_loop(0, nz // chunk, levels, 0)
        return carry

    lax.fori_loop(0, ntr, tracer, 0)

    def react(row, carry):
        mask = wet[pl.ds(row, 1), :]

        def levels(zc, inner):
            zs = pl.ds(pl.multiple_of(zc * chunk, chunk), chunk)
            x = [tt[t, row, zs] for t in range(ntr)]
            for a in range(ntr):
                total = rates[a, 0] * x[0]
                for b in range(1, ntr):
                    total = total + rates[a, b] * x[b]
                reacted = x[a] + (react_step * mask) * total
                tr_out[a, row, zs] = reacted.astype(BF16)
                if a == 0:
                    heat_out[row, zs] = water_atten + chloro_atten * reacted * reacted
            return inner

        lax.fori_loop(0, nz // chunk, levels, 0)
        att = heat_out[row]
        cum = depth_sum(att)
        heating = (mask * light[pl.ds(row, 1), :]) * (jnp.exp(att - cum) - jnp.exp(-cum))
        heat_out[row] = heating
        oc_out[2, row] = oc_out[2, row] + time_step * heating
        return carry

    lax.fori_loop(0, ny, react, 0)

    for index, (dy, dx) in enumerate(DIRS):
        @pl.when(has(dy, dx))
        def _(dy=dy, dx=dx, index=index):
            edge_copy(dy, dx, index).wait_send()
    for side in (0, 1):
        @pl.when(there[2 * side - 1])
        def _(side=side):
            ocean_copy(side).wait_send()
            for t in range(ntr):
                tracer_copy(side, t).wait_send()


def expand_mask(wet_blocks):
    blocks = wet_blocks.astype(F32)
    rows, cols = blocks.shape
    wide = jnp.broadcast_to(blocks[:, None, :, None], (rows, WBY, cols, WBX))
    return wide.reshape(rows * WBY, cols * WBX)


def shards(ngrp, ntile, ocean, tracers, wet_blocks, surface_light, rates):
    ntr, nz, ny, nx = tracers.shape
    vmem = pl.BlockSpec(memory_space=pltpu.VMEM)
    level = (nz, nx)
    outs = pl.pallas_call(
        functools.partial(kernel, ngrp, ntile),
        out_shape=(
            jax.ShapeDtypeStruct((4, ny) + level, F32),
            jax.ShapeDtypeStruct((ntr, ny) + level, BF16),
            jax.ShapeDtypeStruct((ny,) + level, F32),
        ),
        in_specs=[vmem] * 4 + [pl.BlockSpec(memory_space=pltpu.SMEM)],
        out_specs=(vmem,) * 3,
        scratch_shapes=[
            pltpu.VMEM((2, ntr, HALO) + level, BF16),
            pltpu.VMEM((2, len(RIM)) + level, BF16),
            pltpu.VMEM((2, len(RIM)) + level, BF16),
            pltpu.VMEM((3, ny + 4) + level, BF16),
            pltpu.VMEM((2, ny + 4) + level, F32),
            pltpu.VMEM((4, ny + 6) + level, F32),
            pltpu.VMEM((4, ny + 2) + level, F32),
            pltpu.VMEM((ny + 4,) + level, F32),
            pltpu.VMEM((ny + 4,) + level, F32),
            pltpu.VMEM((ny,) + level, F32),
            pltpu.VMEM((ny,) + level, F32),
            pltpu.VMEM((4, ny + 4) + level, F32),
            pltpu.VMEM((2, ny + 5) + level, F32),
            pltpu.VMEM((4, ny) + level, F32),
            pltpu.VMEM((2, ny + 1) + level, F32),
            pltpu.VMEM((ntr, ny) + level, F32),
            pltpu.SemaphoreType.DMA((len(DIRS),)),
            pltpu.SemaphoreType.DMA((len(DIRS),)),
            pltpu.SemaphoreType.DMA((2,)),
            pltpu.SemaphoreType.DMA((2,)),
            pltpu.SemaphoreType.DMA((2, ntr)),
            pltpu.SemaphoreType.DMA((2, ntr)),
        ],
        compiler_params=pltpu.CompilerParams(
            collective_id=0, has_side_effects=True, vmem_limit_bytes=24 * 1024 * 1024
        ),
    )(jnp.swapaxes(tracers, 1, 2), jnp.swapaxes(ocean, 1, 2), expand_mask(wet_blocks), surface_light, rates)
    return jnp.swapaxes(outs[0], 1, 2), jnp.swapaxes(outs[1], 1, 2), jnp.swapaxes(outs[2], 0, 1)


def solution(mesh):
    return jax.shard_map(
        functools.partial(shards, mesh.shape["grp"], mesh.shape["tile"]),
        mesh=mesh,
        in_specs=(
            P(None, None, "grp", "tile"),
            P(None, None, "grp", "tile"),
            P("grp", "tile"),
            P("grp", "tile"),
            P(),
        ),
        out_specs=(
            P(None, None, "grp", "tile"),
            P(None, None, "grp", "tile"),
            P(None, "grp", "tile"),
        ),
        check_vma=False,
    )
```

time: 90.7 us -> 32.8 us (0.36)
  the two profiles are of different devices: /device:TPU:20 before, /device:TPU:1 now
where the time goes in v1:
time: 32.8 us; the launch traced here: 32.6 us
  Pallas kernels  26.9 us (82%)
  local copies, waits for them, and re-layouts  4.25 us (13%)
  other arithmetic  0.7 us (2%)
  between operations  0.69 us (2%)
    pallas_call x1, Pallas kernels, shards(): pl.pallas_call(functools.partial(kernel, ngrp, ntile), out_shape=(jax.Sha...  26.9 us
    unnamed x11, local copies, waits for them, and re-layouts  4.09 us
    broadcast_in_dim x1, other arithmetic, expand_mask(): wide = jnp.broadcast_to(blocks[:, None, :, None], (rows, WBY, cols, WBX))  0.7 us

profile of v1, /device:TPU:1, one launch (start us, length us, event | category | flops | bytes accessed | tf_op | source)
XLA Modules:
  0.0 32.6 jit_solution(13418830450030737579)
XLA Ops:
  0.6 0.0 copy-start.2
  0.6 0.7 %convert_bitcast_fusion = f32[8]{0:T(128)S(1)} fusion(s32[1,8]{1,0:T(1,128)} %param.7), kind=kLoop, calls=%fused_computation.2 | loop fusion | flops 8 | bytes 64 | tf_op jit(solution)/shard_map/broadcast_in_dim | solution.py:410
  1.3 0.1 broadcast_in_dim.13
  1.4 0.1 broadcast_in_dim.14
  1.5 1.0 %copy.16 = f32[4,32,4,128]{3,1,2,0:T(8,128)S(1)} copy(f32[4,32,4,128]{3,2,1,0:T(4,128)} %param.5) | data formatting | bytes 524288 | tf_op args[0]
  2.5 0.0 copy-done.2
  2.5 0.0 copy-start
  2.5 0.0 copy-start.1
  2.5 0.1 copy.15
  2.6 0.6 %copy-done = f32[10,10]{1,0:T(8,128)S(1)} copy-done((f32[10,10]{1,0:T(8,128)S(1)}, f32[10,10]{1,0:T(8,128)}, u32[]{:S(2)}) %copy-start) | copy-done | bytes 424
  3.2 0.0 copy-done.1
  3.2 26.9 %shard_map.76 = (f32[4,4,32,128]{3,2,1,0:T(8,128)S(1)}, bf16[10,4,32,128]{3,2,1,0:T(8,128)(2,1)S(1)}, f32[4,32,128]{2,1,0:T(8,128)S(1)}) custom-call(bf16[10,4,32,128]{3,2,1,0:T(8,128)(2,1)S(1)} %bitcast.11, f32[4,4,32,128]{3,2,1,0:T(8,128)S(1)} %bitcast.12, f32[4,128]{1,0:T(4,128)S(1)} %broadcast_in_dim.15.wet, f32[4,128]{1,0:T(4,128)S(1)} %copy-done.1, ...), custom_call_target="tpu_custom_call" | custom-call | tf_op jit(solution)/shard_map/pallas_call | solution.py:418
  30.1 0.9 %copy.10 = f32[4,32,4,128]{3,2,1,0:T(4,128)} copy(f32[4,32,4,128]{3,1,2,0:T(8,128)S(1)} %bitcast.14) | data formatting | bytes 524288
  31.0 0.9 %copy.11 = bf16[10,32,4,128]{3,2,1,0:T(4,128)(2,1)} copy(bf16[10,32,4,128]{3,1,2,0:T(8,128)(2,1)S(1)} %bitcast.13) | data formatting | bytes 655360
  31.9 0.7 %copy.12 = f32[32,4,128]{2,1,0:T(4,128)} copy(f32[32,4,128]{2,0,1:T(8,128)S(1)} %bitcast.15) | data formatting | bytes 131072
  (1 shorter events, 0.0 us)
Async XLA Ops:
  0.6 1.9 %copy-start.2 = (bf16[10,32,4,128]{3,2,1,0:T(4,128)(2,1)S(1)}, bf16[10,32,4,128]{3,2,1,0:T(4,128)(2,1)}, u32[]{:S(2)}) copy-start(bf16[10,32,4,128]{3,2,1,0:T(4,128)(2,1)} %param.6) | copy-start | bytes 983044
  2.5 0.7 %copy-start = (f32[10,10]{1,0:T(8,128)S(1)}, f32[10,10]{1,0:T(8,128)}, u32[]{:S(2)}) copy-start(f32[10,10]{1,0:T(8,128)} %rates.1) | copy-start | bytes 1204
  2.5 0.7 %copy-start.1 = (f32[4,128]{1,0:T(4,128)S(1)}, f32[4,128]{1,0:T(4,128)}, u32[]{:S(2)}) copy-start(f32[4,128]{1,0:T(4,128)} %light.1) | copy-start | bytes 6148

commit v2 on v1

--- a/solution.py
+++ b/solution.py
@@ -51,12 +51,18 @@
     return x
 
 
-def over_groups(x):
-    step = GROUP
-    while step < x.shape[1]:
-        x = x + lanes(x, step)
-        step *= 2
-    return x
+def loop(steps, at_once, body):
+    at_once = at_once if steps % at_once == 0 else 1
+
+    def some(i, carry):
+        for k in range(at_once):
+            body(at_once * i + k)
+        return carry
+
+    if steps == at_once:
+        some(0, 0)
+    else:
+        lax.fori_loop(0, steps // at_once, some, 0)
 
 
 def split_speed(speed):
@@ -64,8 +70,8 @@
 
 
 def kernel(ngrp, ntile, tr, oc, wet, light, rates, oc_out, tr_out, heat_out,
-           halo_tr, halo_oc, send_oc, px, st, oe, o1, m1, z1, m2, z2, ua, va, ub, vb, tt,
-           p_send, p_recv, o_send, o_recv, t_send, t_recv):
+           halo_tr, halo_oc, send_oc, px, st, wind, oe, o1, m1, z1, m2, z2, ua, va, ub, vb, tt,
+           p_send, p_recv, o_send, o_recv, t_send, t_recv, f_send):
     ntr, ny, nz, nx = tr.shape
     gy, gx = lax.axis_index("grp"), lax.axis_index("tile")
     there = {-1: gy > 0, 0: True, 1: gy < ngrp - 1}
@@ -83,6 +89,12 @@
         def _(dy=dy, dx=dx):
             pl.semaphore_signal(barrier, inc=1, device_id=peer(dy, dx), device_id_type=MESH)
 
+    relay = ngrp % 4 == 0 and ny == HALO
+    place = gy % 4
+    partner = (jnp.where(place < 2, gy + 2, gy - 2), gx)
+    if relay:
+        pl.semaphore_signal(barrier, inc=1, device_id=partner, device_id_type=MESH)
+
     num_y = 1 + there[-1].astype(jnp.int32) + there[1].astype(jnp.int32)
     num_x = 1 + over[-1].astype(jnp.int32) + over[1].astype(jnp.int32)
 
@@ -92,15 +104,14 @@
 
     lane = lane_of((nz, nx))
 
-    def pack(row, carry):
+    def pack(row):
         total = jnp.zeros((nz, nx), F32)
         for field in range(ntr + 4):
             x = tr[field, row].astype(F32) if field < ntr else oc[field - ntr, row]
             total = jnp.where(lane // GROUP == field, lanes(x, GROUP * field + GROUP // 2), total)
         px[1, row + 2] = total.astype(BF16)
-        return carry
-
-    lax.fori_loop(0, ny, pack, 0)
+
+    loop(ny, 1, pack)
 
     def edge_copy(dy, dx, index):
         rows = {-1: (2, ny + 2, 2), 0: (2, 2, ny), 1: (ny, 0, 2)}[dy]
@@ -120,7 +131,27 @@
             send_sem=t_send.at[side, t], recv_sem=t_recv.at[side, t],
             device_id=peer(2 * side - 1, 0), device_id_type=MESH)
 
-    pl.semaphore_wait(barrier, num_y * num_x - 1)
+    def forward_copy(side, t):
+        return pltpu.make_async_remote_copy(
+            src_ref=halo_tr.at[side, t], dst_ref=halo_tr.at[1 - side, t],
+            send_sem=f_send.at[t], recv_sem=t_recv.at[1 - side, t], device_id=partner, device_id_type=MESH)
+
+    def sends(side):
+        direct = there[2 * side - 1]
+        return jnp.logical_and(direct, place != 2 - side) if relay else direct
+
+    def forwards(side):
+        return place == 3 * side
+
+    def forward(t):
+        if relay:
+            for side in (0, 1):
+                @pl.when(forwards(side))
+                def _(side=side):
+                    tracer_copy(side, t).wait_recv()
+                    forward_copy(side, t).start()
+
+    pl.semaphore_wait(barrier, num_y * num_x - 1 + (1 if relay else 0))
     for index, (dy, dx) in enumerate(DIRS):
         @pl.when(has(dy, dx))
         def _(dy=dy, dx=dx, index=index):
@@ -131,7 +162,7 @@
             ocean_copy(side).start()
     for t in range(ntr):
         for side in (0, 1):
-            @pl.when(there[2 * side - 1])
+            @pl.when(sends(side))
             def _(side=side, t=t):
                 tracer_copy(side, t).start()
 
@@ -158,38 +189,46 @@
     part = lane % GROUP
     near_west = part == GROUP // 2
 
-    def strips(slot, carry):
+    group = lane // GROUP
+    source = lax.broadcasted_iota(jnp.int32, (nx, 2 * nx), 0)
+    target = lax.broadcasted_iota(jnp.int32, (nx, 2 * nx), 1)
+    spread = jnp.logical_and(source // GROUP == ntr + target // nx, source % GROUP == target % GROUP)
+    spread = jnp.where(spread, 1.0, 0.0).astype(BF16)
+
+    def strips(slot):
         west, own, east = (px[k, slot].astype(F32) for k in range(3))
         low = part < GROUP // 2
         left = jnp.where(low, west, own)
         right = jnp.where(low, own, east)
         st[0, slot], st[1, slot] = left, right
+        for side, x in enumerate((left, right)):
+            both = jnp.dot(x.astype(BF16), spread, preferred_element_type=F32)
+            wind[side, 0, slot], wind[side, 1, slot] = both[:, :nx], both[:, nx:]
         mid = jnp.where(near_west, lanes(left, 1), lanes(right, -1))
         far = jnp.where(near_west, lanes(left, 2), lanes(right, -2))
         close = jnp.where(near_west, left, right)
         m1[slot] = mid
         z1[slot] = mid + 0.5 * minmod(mid - far, close - mid)
-        return carry
-
-    lax.fori_loop(0, ny + 4, strips, 0)
-
-    group = lane // GROUP
-    buoyancy = jnp.where(group == ntr + 2, thermal, 0.0) - jnp.where(group == ntr + 3, haline, 0.0)
+
+    loop(ny + 4, 4, strips)
+    forward(0)
+
     blend = jnp.where(group < ntr + 2, viscosity, diffusion)
 
     def strip_step(side, slot):
         c = [st[side, slot + k] for k in (-2, -1, 0, 1, 2)]
         mid = c[2]
-        zonal = over_groups(jnp.where(group == ntr, mid, 0.0))
-        merid = [over_groups(jnp.where(group == ntr + 1, x, 0.0)) for x in c[1:4]]
+        zonal = wind[side, 0, slot]
+        merid = [wind[side, 1, slot + k] for k in (-1, 0, 1)]
         east, west, north, south = lanes(mid, -1), lanes(mid, 1), c[3], c[1]
         gx_, gy_ = 0.5 * (east - west), 0.5 * (north - south)
         lap = east + west + north + south - 4.0 * mid
-        px_ = gravity_red * depth_sum(over_groups(buoyancy * gx_))
-        py_ = gravity_red * depth_sum(over_groups(buoyancy * gy_))
+        force = jnp.where(group == ntr, thermal * lanes(gx_, -2 * GROUP) - haline * lanes(gx_, -3 * GROUP),
+                          thermal * lanes(gy_, -GROUP) - haline * lanes(gy_, -2 * GROUP))
+        press = gravity_red * depth_sum(force)
         rate = blend * lap - (zonal * gx_ + merid[1] * gy_)
-        rate = rate + jnp.where(group == ntr, coriolis * merid[1] - px_, 0.0)
-        rate = rate - jnp.where(group == ntr + 1, coriolis * zonal + py_, 0.0)
+        rate = rate + jnp.where(group == ntr, coriolis * merid[1] - press, 0.0)
+        rate = rate - jnp.where(group == ntr + 1, coriolis * zonal + press, 0.0)
         ocean_one = mid + time_step * rate
         diff = mid - west
         half = 0.5 * minmod(diff, lanes(diff, -1))
@@ -209,7 +248,7 @@
     in_west = jnp.where(over[-1], 1.0, 0.0)
     in_east = jnp.where(over[1], 1.0, 0.0)
 
-    def strip_row(row, carry):
+    def strip_row(row):
         left = strip_step(0, row + 2)
         right = strip_step(1, row + 2)
         mid = jnp.where(near_west, in_west * lanes(left, 1), in_east * lanes(right, -1))
@@ -217,9 +256,9 @@
         close = jnp.where(near_west, left, right)
         m2[row] = mid
         z2[row] = mid + 0.5 * minmod(mid - far, close - mid)
-        return carry
-
-    lax.fori_loop(0, ny, strip_row, 0)
+
+    loop(ny, 2, strip_row)
+    forward(1)
 
     for side in (0, 1):
         @pl.when(there[1 - 2 * side])
@@ -256,22 +295,23 @@
     in_south = jnp.where(there[-1], 1.0, 0.0)
     in_north = jnp.where(there[1], 1.0, 0.0)
 
-    def ocean_first(k, carry):
+    def ocean_first(k):
         keep = jnp.where(k == 0, in_south, jnp.where(k == ny + 1, in_north, 1.0))
         rate = ocean_rates(lambda f, dy: oe[f, k + 2 + dy], m1[k + 1])
         for f in range(4):
             o1[f, k] = keep * (oe[f, k + 2] + time_step * rate[f])
-        return carry
-
-    lax.fori_loop(0, ny + 2, ocean_first, 0)
-
-    def ocean_second(row, carry):
+
+    loop(ny + 2, 2, ocean_first)
+    for t in (2, 3):
+        forward(t)
+
+    def ocean_second(row):
         rate = ocean_rates(lambda f, dy: o1[f, row + 1 + dy], m2[row])
         for f in range(4):
             oc_out[f, row] = 0.5 * (oe[f, row + 3] + o1[f, row + 1] + time_step * rate[f])
-        return carry
-
-    lax.fori_loop(0, ny, ocean_second, 0)
+
+    loop(ny, 2, ocean_second)
+    forward(4)
 
     def zonal_faces(scale, mid, edge):
         rim = lanes(edge, shift_back(ntr))
@@ -279,32 +319,30 @@
         west = jnp.where(first, rim, lanes(mid, 1))
         return split_speed(scale * (west + mid)) + split_speed(scale * (mid + east))
 
-    def faces_first(j, carry):
+    def faces_first(j):
         for k, x in enumerate(zonal_faces(0.5 * time_step, oe[0, j + 1], m1[j])):
             ua[k, j] = x
-        return carry
-
-    lax.fori_loop(0, ny + 4, faces_first, 0)
-
-    def faces_second(j, carry):
+
+    loop(ny + 4, 4, faces_first)
+
+    def faces_second(j):
         for k, x in enumerate(zonal_faces(0.25 * time_step, o1[0, j + 1], m2[j])):
             ub[k, j] = x
-        return carry
-
-    lax.fori_loop(0, ny, faces_second, 0)
-
-    def merid_first(j, carry):
+
+    loop(ny, 4, faces_second)
+
+    def merid_first(j):
         va[0, j], va[1, j] = split_speed((0.5 * time_step) * (oe[1, j] + oe[1, j + 1]))
-        return carry
-
-    lax.fori_loop(0, ny + 5, merid_first, 0)
-
-    def merid_second(j, carry):
+
+    loop(ny + 5, 3, merid_first)
+
+    def merid_second(j):
         vb[0, j], vb[1, j] = split_speed((0.25 * time_step) * (o1[1, j] + o1[1, j + 1]))
-        return carry
-
-    lax.fori_loop(0, ny + 1, merid_second, 0)
-
+
+    loop(ny + 1, 5, merid_second)
+
+    forward(5)
+    ahead = 6
     chunk = 16
     clane = lane_of((chunk, nx))
     cfirst, clast = clane == 0, clane == nx - 1
@@ -329,13 +367,17 @@
 
     def tracer(t, carry):
         for side in (0, 1):
-            @pl.when(there[1 - 2 * side])
+            arrives = there[1 - 2 * side]
+            if relay:
+                arrives = jnp.logical_and(arrives, jnp.logical_not(forwards(side)))
+
+            @pl.when(arrives)
             def _(side=side):
                 tracer_copy(side, t).wait_recv()
         back = nx - (GROUP * t + GROUP // 2)
 
-        def levels(zc, inner):
-            zs = pl.ds(pl.multiple_of(zc * chunk, chunk), chunk)
+        def levels(zc):
+            zs = pl.ds(zc * chunk, chunk)
             c = [halo_tr[1, t, k, zs].astype(F32) for k in range(HALO)]
             c += [tr[t, k, zs].astype(F32) for k in range(ny)]
             c += [halo_tr[0, t, k, zs].astype(F32) for k in range(HALO)]
@@ -359,9 +401,13 @@
                 mid = one[j + 2]
                 div = zonal_part(mid, rim, rim_value, [ub[k, j, zs] for k in range(4)]) + along_y[j]
                 tt[t, j, zs] = 0.5 * (c[j + 4] + mid) - div
-            return inner
-
-        lax.fori_loop(0, nz // chunk, levels, 0)
+
+        for zc in range(nz // chunk):
+            levels(zc)
+        if relay:
+            @pl.when(t + ahead < ntr)
+            def _():
+                forward(t + ahead)
         return carry
 
     lax.fori_loop(0, ntr, tracer, 0)
@@ -400,8 +446,17 @@
         @pl.when(there[2 * side - 1])
         def _(side=side):
             ocean_copy(side).wait_send()
+
+        @pl.when(sends(side))
+        def _(side=side):
             for t in range(ntr):
                 tracer_copy(side, t).wait_send()
+
+        if relay:
+            @pl.when(forwards(side))
+            def _(side=side):
+                for t in range(ntr):
+                    forward_copy(side, t).wait_send()
 
 
 def expand_mask(wet_blocks):
@@ -430,6 +485,7 @@
             pltpu.VMEM((2, len(RIM)) + level, BF16),
             pltpu.VMEM((3, ny + 4) + level, BF16),
             pltpu.VMEM((2, ny + 4) + level, F32),
+            pltpu.VMEM((2, 2, ny + 4) + level, F32),
             pltpu.VMEM((4, ny + 6) + level, F32),
             pltpu.VMEM((4, ny + 2) + level, F32),
             pltpu.VMEM((ny + 4,) + level, F32),
@@ -447,6 +503,7 @@
             pltpu.SemaphoreType.DMA((2,)),
             pltpu.SemaphoreType.DMA((2, ntr)),
             pltpu.SemaphoreType.DMA((2, ntr)),
+            pltpu.SemaphoreType.DMA((ntr,)),
         ],
         compiler_params=pltpu.CompilerParams(
             collective_id=0, has_side_effects=True, vmem_limit_bytes=24 * 1024 * 1024

time: 32.8 us -> 30.2 us (0.921)
  Pallas kernels: 26.9 us -> 24.3 us
    pallas_call x1, Pallas kernels: 26.9 us -> 24.3 us  [shards(): pl.pallas_call(functools.partial(kernel, ngrp, ntile), out_shape=(jax.Sha...]
where the time goes in v2:
time: 30.2 us; the launch traced here: 30 us
  Pallas kernels  24.3 us (80%)
  local copies, waits for them, and re-layouts  4.25 us (14%)
  other arithmetic  0.7 us (2%)
  between operations  0.69 us (2%)
    pallas_call x1, Pallas kernels, shards(): pl.pallas_call(functools.partial(kernel, ngrp, ntile), out_shape=(jax.Sha...  24.3 us
    unnamed x11, local copies, waits for them, and re-layouts  4.09 us
    broadcast_in_dim x1, other arithmetic, expand_mask(): wide = jnp.broadcast_to(blocks[:, None, :, None], (rows, WBY, cols, WBX))  0.7 us

profile of v2, /device:TPU:1, one launch (start us, length us, event | category | flops | bytes accessed | tf_op | source)
XLA Modules:
  0.0 30.0 jit_solution(5724822401500289934)
XLA Ops:
  0.6 0.0 copy-start.2
  0.6 0.7 %convert_bitcast_fusion = f32[8]{0:T(128)S(1)} fusion(s32[1,8]{1,0:T(1,128)} %param.7), kind=kLoop, calls=%fused_computation.2 | loop fusion | flops 8 | bytes 64 | tf_op jit(solution)/shard_map/broadcast_in_dim | solution.py:465
  1.3 0.1 broadcast_in_dim.13
  1.4 0.1 broadcast_in_dim.14
  1.5 1.0 %copy.16 = f32[4,32,4,128]{3,1,2,0:T(8,128)S(1)} copy(f32[4,32,4,128]{3,2,1,0:T(4,128)} %param.5) | data formatting | bytes 524288 | tf_op args[0]
  2.5 0.0 copy-done.2
  2.5 0.0 copy-start
  2.5 0.0 copy-start.1
  2.5 0.1 copy.15
  2.6 0.6 %copy-done = f32[10,10]{1,0:T(8,128)S(1)} copy-done((f32[10,10]{1,0:T(8,128)S(1)}, f32[10,10]{1,0:T(8,128)}, u32[]{:S(2)}) %copy-start) | copy-done | bytes 424
  3.2 0.0 copy-done.1
  3.2 24.3 %shard_map.76 = (f32[4,4,32,128]{3,2,1,0:T(8,128)S(1)}, bf16[10,4,32,128]{3,2,1,0:T(8,128)(2,1)S(1)}, f32[4,32,128]{2,1,0:T(8,128)S(1)}) custom-call(bf16[10,4,32,128]{3,2,1,0:T(8,128)(2,1)S(1)} %bitcast.11, f32[4,4,32,128]{3,2,1,0:T(8,128)S(1)} %bitcast.12, f32[4,128]{1,0:T(4,128)S(1)} %broadcast_in_dim.15.wet, f32[4,128]{1,0:T(4,128)S(1)} %copy-done.1, ...), custom_call_target="tpu_custom_call" | custom-call | tf_op jit(solution)/shard_map/pallas_call | solution.py:473
  27.5 0.9 %copy.10 = f32[4,32,4,128]{3,2,1,0:T(4,128)} copy(f32[4,32,4,128]{3,1,2,0:T(8,128)S(1)} %bitcast.14) | data formatting | bytes 524288
  28.4 0.9 %copy.11 = bf16[10,32,4,128]{3,2,1,0:T(4,128)(2,1)} copy(bf16[10,32,4,128]{3,1,2,0:T(8,128)(2,1)S(1)} %bitcast.13) | data formatting | bytes 655360
  29.3 0.7 %copy.12 = f32[32,4,128]{2,1,0:T(4,128)} copy(f32[32,4,128]{2,0,1:T(8,128)S(1)} %bitcast.15) | data formatting | bytes 131072
  (1 shorter events, 0.0 us)
Async XLA Ops:
  0.6 1.9 %copy-start.2 = (bf16[10,32,4,128]{3,2,1,0:T(4,128)(2,1)S(1)}, bf16[10,32,4,128]{3,2,1,0:T(4,128)(2,1)}, u32[]{:S(2)}) copy-start(bf16[10,32,4,128]{3,2,1,0:T(4,128)(2,1)} %param.6) | copy-start | bytes 983044
  2.5 0.7 %copy-start = (f32[10,10]{1,0:T(8,128)S(1)}, f32[10,10]{1,0:T(8,128)}, u32[]{:S(2)}) copy-start(f32[10,10]{1,0:T(8,128)} %rates.1) | copy-start | bytes 1204
  2.5 0.7 %copy-start.1 = (f32[4,128]{1,0:T(4,128)S(1)}, f32[4,128]{1,0:T(4,128)}, u32[]{:S(2)}) copy-start(f32[4,128]{1,0:T(4,128)} %light.1) | copy-start | bytes 6148

commit v3 on v2

--- a/solution.py
+++ b/solution.py
@@ -31,7 +31,7 @@
 
 
 def minmod(a, b):
-    return jnp.maximum(jnp.minimum(a, b), 0.0) + jnp.minimum(jnp.maximum(a, b), 0.0)
+    return jnp.minimum(jnp.maximum(a, jnp.minimum(b, 0.0)), jnp.maximum(b, 0.0))
 
 
 def lanes(x, shift):
@@ -69,10 +69,15 @@
     return jnp.maximum(speed, 0.0), jnp.minimum(speed, 0.0)
 
 
-def kernel(ngrp, ntile, tr, oc, wet, light, rates, oc_out, tr_out, heat_out,
-           halo_tr, halo_oc, send_oc, px, st, wind, oe, o1, m1, z1, m2, z2, ua, va, ub, vb, tt,
+def kernel(ngrp, ntile, ny, tr, oc, wet, light, rates, oc_out, tr_out, heat_out,
+           halo_tr, halo_oc, send_oc, px, st, wind, oe, o1, m1, z1, m2, z2, ua, va, ub, vb, tt, plain, around,
            p_send, p_recv, o_send, o_recv, t_send, t_recv, f_send):
-    ntr, ny, nz, nx = tr.shape
+    ntr, cells, nx = tr.shape
+    nz = cells // ny
+
+    def spot(row, level=0, count=nz):
+        return pl.ds(level * ny + row, count, stride=ny)
+
     gy, gx = lax.axis_index("grp"), lax.axis_index("tile")
     there = {-1: gy > 0, 0: True, 1: gy < ngrp - 1}
     over = {-1: gx > 0, 0: True, 1: gx < ntile - 1}
@@ -89,7 +94,7 @@
         def _(dy=dy, dx=dx):
             pl.semaphore_signal(barrier, inc=1, device_id=peer(dy, dx), device_id_type=MESH)
 
-    relay = ngrp % 4 == 0 and ny == HALO
+    relay = ngrp % 4 == 0
     place = gy % 4
     partner = (jnp.where(place < 2, gy + 2, gy - 2), gx)
     if relay:
@@ -98,16 +103,24 @@
     num_y = 1 + there[-1].astype(jnp.int32) + there[1].astype(jnp.int32)
     num_x = 1 + over[-1].astype(jnp.int32) + over[1].astype(jnp.int32)
 
+    for field in range(4):
+        for row in range(ny):
+            oe[field, row + 3] = oc[field, spot(row), :]
     for slot, (field, depth) in enumerate(RIM):
-        send_oc[1, slot] = oc[field, ny - depth].astype(BF16)
-        send_oc[0, slot] = oc[field, depth - 1].astype(BF16)
+        send_oc[1, slot] = oe[field, ny + 3 - depth].astype(BF16)
+        send_oc[0, slot] = oe[field, depth + 2].astype(BF16)
 
     lane = lane_of((nz, nx))
+
+    def unfold(t):
+        plain[t] = tr[t].astype(F32)
+
+    loop(ntr, 2, unfold)
 
     def pack(row):
         total = jnp.zeros((nz, nx), F32)
         for field in range(ntr + 4):
-            x = tr[field, row].astype(F32) if field < ntr else oc[field - ntr, row]
+            x = plain[field, spot(row), :] if field < ntr else oe[field - ntr, row + 3]
             total = jnp.where(lane // GROUP == field, lanes(x, GROUP * field + GROUP // 2), total)
         px[1, row + 2] = total.astype(BF16)
 
@@ -127,7 +140,7 @@
 
     def tracer_copy(side, t):
         return pltpu.make_async_remote_copy(
-            src_ref=tr.at[t, pl.ds(side * (ny - HALO), HALO)], dst_ref=halo_tr.at[side, t],
+            src_ref=tr.at[t], dst_ref=halo_tr.at[side, t],
             send_sem=t_send.at[side, t], recv_sem=t_recv.at[side, t],
             device_id=peer(2 * side - 1, 0), device_id_type=MESH)
 
@@ -176,10 +189,6 @@
         def _(side=side):
             halo_oc[side] = jnp.zeros(halo_oc.shape[1:], BF16)
             halo_tr[side] = jnp.zeros(halo_tr.shape[1:], BF16)
-
-    for field in range(4):
-        for row in range(ny):
-            oe[field, row + 3] = oc[field, row]
 
     for index, (dy, dx) in enumerate(DIRS):
         @pl.when(has(-dy, -dx))
@@ -257,7 +266,7 @@
         m2[row] = mid
         z2[row] = mid + 0.5 * minmod(mid - far, close - mid)
 
-    loop(ny, 2, strip_row)
+    loop(ny, 4, strip_row)
     forward(1)
 
     for side in (0, 1):
@@ -301,16 +310,16 @@
         for f in range(4):
             o1[f, k] = keep * (oe[f, k + 2] + time_step * rate[f])
 
-    loop(ny + 2, 2, ocean_first)
+    loop(ny + 2, 3, ocean_first)
     for t in (2, 3):
         forward(t)
 
     def ocean_second(row):
         rate = ocean_rates(lambda f, dy: o1[f, row + 1 + dy], m2[row])
         for f in range(4):
-            oc_out[f, row] = 0.5 * (oe[f, row + 3] + o1[f, row + 1] + time_step * rate[f])
-
-    loop(ny, 2, ocean_second)
+            oc_out[f, spot(row), :] = 0.5 * (oe[f, row + 3] + o1[f, row + 1] + time_step * rate[f])
+
+    loop(ny, 4, ocean_second)
     forward(4)
 
     def zonal_faces(scale, mid, edge):
@@ -374,13 +383,15 @@
             @pl.when(arrives)
             def _(side=side):
                 tracer_copy(side, t).wait_recv()
+        for side in (0, 1):
+            around[side] = halo_tr[side, t].astype(F32)
         back = nx - (GROUP * t + GROUP // 2)
 
         def levels(zc):
             zs = pl.ds(zc * chunk, chunk)
-            c = [halo_tr[1, t, k, zs].astype(F32) for k in range(HALO)]
-            c += [tr[t, k, zs].astype(F32) for k in range(ny)]
-            c += [halo_tr[0, t, k, zs].astype(F32) for k in range(HALO)]
+            c = [around[1, spot(k + ny - HALO, zc * chunk, chunk), :] for k in range(HALO)]
+            c += [plain[t, spot(k, zc * chunk, chunk), :] for k in range(ny)]
+            c += [around[0, spot(k, zc * chunk, chunk), :] for k in range(HALO)]
             along_y = merid_part(c, lambda k: (va[0, k, zs], va[1, k, zs]))
             one = []
             for j in range(ny + 4):
@@ -412,31 +423,36 @@
 
     lax.fori_loop(0, ntr, tracer, 0)
 
-    def react(row, carry):
-        mask = wet[pl.ds(row, 1), :]
-
-        def levels(zc, inner):
-            zs = pl.ds(pl.multiple_of(zc * chunk, chunk), chunk)
+    def react(row):
+        mask = react_step * wet[pl.ds(row, 1), :]
+
+        for zc in range(nz // chunk):
+            zs = pl.ds(zc * chunk, chunk)
             x = [tt[t, row, zs] for t in range(ntr)]
             for a in range(ntr):
                 total = rates[a, 0] * x[0]
                 for b in range(1, ntr):
                     total = total + rates[a, b] * x[b]
-                reacted = x[a] + (react_step * mask) * total
-                tr_out[a, row, zs] = reacted.astype(BF16)
+                reacted = x[a] + mask * total
+                plain[a, spot(row, zc * chunk, chunk), :] = reacted
                 if a == 0:
-                    heat_out[row, zs] = water_atten + chloro_atten * reacted * reacted
-            return inner
-
-        lax.fori_loop(0, nz // chunk, levels, 0)
-        att = heat_out[row]
+                    tt[0, row, zs] = water_atten + chloro_atten * reacted * reacted
+
+    loop(ny, 1, react)
+
+    def heat(row):
+        att = tt[0, row]
         cum = depth_sum(att)
-        heating = (mask * light[pl.ds(row, 1), :]) * (jnp.exp(att - cum) - jnp.exp(-cum))
-        heat_out[row] = heating
-        oc_out[2, row] = oc_out[2, row] + time_step * heating
-        return carry
-
-    lax.fori_loop(0, ny, react, 0)
+        heating = (wet[pl.ds(row, 1), :] * light[pl.ds(row, 1), :]) * (jnp.exp(att - cum) - jnp.exp(-cum))
+        heat_out[spot(row), :] = heating
+        oc_out[2, spot(row), :] = oc_out[2, spot(row), :] + time_step * heating
+
+    loop(ny, 4, heat)
+
+    def fold(t):
+        tr_out[t] = plain[t].astype(BF16)
+
+    loop(ntr, 2, fold)
 
     for index, (dy, dx) in enumerate(DIRS):
         @pl.when(has(dy, dx))
@@ -469,18 +485,18 @@
 def shards(ngrp, ntile, ocean, tracers, wet_blocks, surface_light, rates):
     ntr, nz, ny, nx = tracers.shape
     vmem = pl.BlockSpec(memory_space=pltpu.VMEM)
-    level = (nz, nx)
+    level, flat = (nz, nx), (nz * ny, nx)
     outs = pl.pallas_call(
-        functools.partial(kernel, ngrp, ntile),
+        functools.partial(kernel, ngrp, ntile, ny),
         out_shape=(
-            jax.ShapeDtypeStruct((4, ny) + level, F32),
-            jax.ShapeDtypeStruct((ntr, ny) + level, BF16),
-            jax.ShapeDtypeStruct((ny,) + level, F32),
+            jax.ShapeDtypeStruct((4,) + flat, F32),
+            jax.ShapeDtypeStruct((ntr,) + flat, BF16),
+            jax.ShapeDtypeStruct(flat, F32),
         ),
         in_specs=[vmem] * 4 + [pl.BlockSpec(memory_space=pltpu.SMEM)],
         out_specs=(vmem,) * 3,
         scratch_shapes=[
-            pltpu.VMEM((2, ntr, HALO) + level, BF16),
+            pltpu.VMEM((2, ntr) + flat, BF16),
             pltpu.VMEM((2, len(RIM)) + level, BF16),
             pltpu.VMEM((2, len(RIM)) + level, BF16),
             pltpu.VMEM((3, ny + 4) + level, BF16),
@@ -497,6 +513,8 @@
             pltpu.VMEM((4, ny) + level, F32),
             pltpu.VMEM((2, ny + 1) + level, F32),
             pltpu.VMEM((ntr, ny) + level, F32),
+            pltpu.VMEM((ntr,) + flat, F32),
+            pltpu.VMEM((2,) + flat, F32),
             pltpu.SemaphoreType.DMA((len(DIRS),)),
             pltpu.SemaphoreType.DMA((len(DIRS),)),
             pltpu.SemaphoreType.DMA((2,)),
@@ -508,8 +526,8 @@
         compiler_params=pltpu.CompilerParams(
             collective_id=0, has_side_effects=True, vmem_limit_bytes=24 * 1024 * 1024
         ),
-    )(jnp.swapaxes(tracers, 1, 2), jnp.swapaxes(ocean, 1, 2), expand_mask(wet_blocks), surface_light, rates)
-    return jnp.swapaxes(outs[0], 1, 2), jnp.swapaxes(outs[1], 1, 2), jnp.swapaxes(outs[2], 0, 1)
+    )(tracers.reshape((ntr,) + flat), ocean.reshape((4,) + flat), expand_mask(wet_blocks), surface_light, rates)
+    return outs[0].reshape(ocean.shape), outs[1].reshape(tracers.shape), outs[2].reshape(ocean.shape[1:])
 
 
 def solution(mesh):

time: 30.2 us -> 30.7 us (1.017)
  local copies, waits for them, and re-layouts: 4.25 us -> 5.45 us
  other arithmetic: 0.7 us -> 0.01 us
    unnamed x11 -> x13, local copies, waits for them, and re-layouts: 4.09 us -> 5.29 us
    broadcast_in_dim x1, other arithmetic: 0.7 us -> 0.01 us  [expand_mask(): wide = jnp.broadcast_to(blocks[:, None, :, None], (rows, WBY, cols, WBX))]
where the time goes in v3:
time: 30.7 us; the launch traced here: 30.5 us
  Pallas kernels  24.3 us (79%)
  local copies, waits for them, and re-layouts  5.45 us (18%)
  between operations  0.67 us (2%)
    pallas_call x1, Pallas kernels, shards(): pl.pallas_call(functools.partial(kernel, ngrp, ntile, ny), out_shape=(jax...  24.3 us
    unnamed x13, local copies, waits for them, and re-layouts  5.29 us

profile of v3, /device:TPU:1, one launch (start us, length us, event | category | flops | bytes accessed | tf_op | source)
XLA Modules:
  0.0 30.5 jit_solution(7160621723528163810)
XLA Ops:
  0.6 0.0 copy-start.4
  0.6 0.0 copy-start.2
  0.7 0.6 %copy-done.4 = s32[1,8]{1,0:T(1,128)S(1)} copy-done((s32[1,8]{1,0:T(1,128)S(1)}, s32[1,8]{1,0:T(1,128)}, u32[]{:S(2)}) %copy-start.4) | copy-done | bytes 56
  1.3 0.1 broadcast_in_dim.13
  1.4 0.1 broadcast_in_dim.14
  1.4 0.0 copy-start.3
  1.5 0.0 copy-done.2
  1.5 0.7 %copy-done.3 = f32[4,128]{1,0:T(4,128)S(1)} copy-done((f32[4,128]{1,0:T(4,128)S(1)}, f32[4,128]{1,0:T(4,128)}, u32[]{:S(2)}) %copy-start.3) | copy-done | bytes 2072
  2.1 0.0 copy-start
  2.1 1.0 %copy-done = bf16[10,32,4,128]{3,2,1,0:T(4,128)(2,1)S(1)} copy-done((bf16[10,32,4,128]{3,2,1,0:T(4,128)(2,1)S(1)}, bf16[10,32,4,128]{3,2,1,0:T(4,128)(2,1)}, u32[]{:S(2)}) %copy-start) | copy-done | bytes 327704
  3.1 0.0 copy-start.1
  3.1 0.9 %copy-done.1 = f32[4,32,4,128]{3,2,1,0:T(4,128)S(1)} copy-done((f32[4,32,4,128]{3,2,1,0:T(4,128)S(1)}, f32[4,32,4,128]{3,2,1,0:T(4,128)}, u32[]{:S(2)}) %copy-start.1) | copy-done | bytes 262168
  4.1 24.3 %shard_map.76 = (f32[4,128,128]{2,1,0:T(8,128)S(1)}, bf16[10,128,128]{2,1,0:T(8,128)(2,1)S(1)}, f32[128,128]{1,0:T(8,128)S(1)}) custom-call(bf16[10,128,128]{2,1,0:T(8,128)(2,1)S(1)} %bitcast.7, f32[4,128,128]{2,1,0:T(8,128)S(1)} %bitcast.9, f32[4,128]{1,0:T(4,128)S(1)} %broadcast_in_dim.15.wet, f32[4,128]{1,0:T(4,128)S(1)} %copy-done.3, f32[10,10]{1,0:T(8,128)S(1)} %copy-done.2), custom_call_target="tpu_custom_call" | custom-call | tf_op jit(solution)/shard_map/pallas_call | solution.py:489
  28.4 0.7 %copy.11 = f32[4,32,4,128]{3,2,1,0:T(4,128)} copy(f32[4,32,4,128]{3,2,1,0:T(4,128)S(1)} %bitcast.10) | data formatting | bytes 524288
  29.1 0.7 %copy.12 = bf16[10,32,4,128]{3,2,1,0:T(4,128)(2,1)} copy(bf16[10,32,4,128]{3,2,1,0:T(4,128)(2,1)S(1)} %bitcast.8) | data formatting | bytes 655360
  29.8 0.6 %copy.13 = f32[32,4,128]{2,1,0:T(4,128)} copy(f32[32,4,128]{2,1,0:T(4,128)S(1)} %bitcast.11) | data formatting | bytes 131072
  (2 shorter events, 0.0 us)
Async XLA Ops:
  0.6 0.7 %copy-start.4 = (s32[1,8]{1,0:T(1,128)S(1)}, s32[1,8]{1,0:T(1,128)}, u32[]{:S(2)}) copy-start(s32[1,8]{1,0:T(1,128)} %param.7) | copy-start | bytes 100
  0.6 0.8 %copy-start.2 = (f32[10,10]{1,0:T(8,128)S(1)}, f32[10,10]{1,0:T(8,128)}, u32[]{:S(2)}) copy-start(f32[10,10]{1,0:T(8,128)} %rates.1) | copy-start | bytes 1204
  1.4 0.7 %copy-start.3 = (f32[4,128]{1,0:T(4,128)S(1)}, f32[4,128]{1,0:T(4,128)}, u32[]{:S(2)}) copy-start(f32[4,128]{1,0:T(4,128)} %light.1) | copy-start | bytes 6148
  2.1 1.0 %copy-start = (bf16[10,32,4,128]{3,2,1,0:T(4,128)(2,1)S(1)}, bf16[10,32,4,128]{3,2,1,0:T(4,128)(2,1)}, u32[]{:S(2)}) copy-start(bf16[10,32,4,128]{3,2,1,0:T(4,128)(2,1)} %param.6) | copy-start | bytes 983044
  3.1 0.9 %copy-start.1 = (f32[4,32,4,128]{3,2,1,0:T(4,128)S(1)}, f32[4,32,4,128]{3,2,1,0:T(4,128)}, u32[]{:S(2)}) copy-start(f32[4,32,4,128]{3,2,1,0:T(4,128)} %param.5) | copy-start | bytes 786436

commit v4 on v3

--- a/solution.py
+++ b/solution.py
@@ -21,6 +21,7 @@
 water_atten = 0.3
 chloro_atten = 0.2
 
+VMEM_GRANT = 64000 * 1024
 MESH = pl.DeviceIdType.MESH
 F32 = jnp.float32
 BF16 = jnp.bfloat16
@@ -69,8 +70,8 @@
     return jnp.maximum(speed, 0.0), jnp.minimum(speed, 0.0)
 
 
-def kernel(ngrp, ntile, ny, tr, oc, wet, light, rates, oc_out, tr_out, heat_out,
-           halo_tr, halo_oc, send_oc, px, st, wind, oe, o1, m1, z1, m2, z2, ua, va, ub, vb, tt, plain, around,
+def kernel(ngrp, ntile, ny, tr_in, oc_in, wet_in, light_in, rates_in, oc_final, tr_final, heat_final,
+           oc_out, tr_out, heat_out, out_sem, tr, oc, wet, light, rates, in_sem, halo_tr, halo_oc, send_oc, px, st, wind, oe, o1, m1, z1, m2, z2, ua, va, ub, vb, tt, plain, around,
            p_send, p_recv, o_send, o_recv, t_send, t_recv, f_send):
     ntr, cells, nx = tr.shape
     nz = cells // ny
@@ -79,6 +80,10 @@
         return pl.ds(level * ny + row, count, stride=ny)
 
     gy, gx = lax.axis_index("grp"), lax.axis_index("tile")
+    inputs = [pltpu.make_async_copy(src, dst, in_sem.at[k]) for k, (src, dst) in enumerate(
+        [(oc_in, oc), (tr_in, tr), (wet_in, wet), (light_in, light), (rates_in, rates)])]
+    for copy in inputs:
+        copy.start()
     there = {-1: gy > 0, 0: True, 1: gy < ngrp - 1}
     over = {-1: gx > 0, 0: True, 1: gx < ntile - 1}
 
@@ -103,6 +108,7 @@
     num_y = 1 + there[-1].astype(jnp.int32) + there[1].astype(jnp.int32)
     num_x = 1 + over[-1].astype(jnp.int32) + over[1].astype(jnp.int32)
 
+    inputs[0].wait()
     for field in range(4):
         for row in range(ny):
             oe[field, row + 3] = oc[field, spot(row), :]
@@ -111,6 +117,8 @@
         send_oc[0, slot] = oe[field, depth + 2].astype(BF16)
 
     lane = lane_of((nz, nx))
+
+    inputs[1].wait()
 
     def unfold(t):
         plain[t] = tr[t].astype(F32)
@@ -267,7 +275,8 @@
         z2[row] = mid + 0.5 * minmod(mid - far, close - mid)
 
     loop(ny, 4, strip_row)
-    forward(1)
+    for t in (1, 2):
+        forward(t)
 
     for side in (0, 1):
         @pl.when(there[1 - 2 * side])
@@ -311,7 +320,7 @@
             o1[f, k] = keep * (oe[f, k + 2] + time_step * rate[f])
 
     loop(ny + 2, 3, ocean_first)
-    for t in (2, 3):
+    for t in (3, 4):
         forward(t)
 
     def ocean_second(row):
@@ -320,7 +329,12 @@
             oc_out[f, spot(row), :] = 0.5 * (oe[f, row + 3] + o1[f, row + 1] + time_step * rate[f])
 
     loop(ny, 4, ocean_second)
-    forward(4)
+    results = [pltpu.make_async_copy(oc_out.at[f], oc_final.at[f], out_sem.at[f]) for f in range(4)]
+    results.append(pltpu.make_async_copy(tr_out, tr_final, out_sem.at[4]))
+    results.append(pltpu.make_async_copy(heat_out, heat_final, out_sem.at[5]))
+    for f in (0, 1, 3):
+        results[f].start()
+    forward(5)
 
     def zonal_faces(scale, mid, edge):
         rim = lanes(edge, shift_back(ntr))
@@ -350,8 +364,8 @@
 
     loop(ny + 1, 5, merid_second)
 
-    forward(5)
-    ahead = 6
+    forward(6)
+    ahead = 7
     chunk = 16
     clane = lane_of((chunk, nx))
     cfirst, clast = clane == 0, clane == nx - 1
@@ -423,8 +437,18 @@
 
     lax.fori_loop(0, ntr, tracer, 0)
 
+    for copy in inputs[2:]:
+        copy.wait()
+    block = lane_of((1, nx)) // WBX
+
+    def wet_row(row):
+        total = jnp.zeros((1, nx), F32)
+        for k in range(nx // WBX):
+            total = jnp.where(block == k, wet[row // WBY, k].astype(F32), total)
+        return total
+
     def react(row):
-        mask = react_step * wet[pl.ds(row, 1), :]
+        mask = react_step * wet_row(row)
 
         for zc in range(nz // chunk):
             zs = pl.ds(zc * chunk, chunk)
@@ -438,21 +462,24 @@
                 if a == 0:
                     tt[0, row, zs] = water_atten + chloro_atten * reacted * reacted
 
-    loop(ny, 1, react)
+    loop(ny, 2, react)
+
+    def fold(t):
+        tr_out[t] = plain[t].astype(BF16)
+
+    loop(ntr, 2, fold)
+    results[4].start()
 
     def heat(row):
         att = tt[0, row]
         cum = depth_sum(att)
-        heating = (wet[pl.ds(row, 1), :] * light[pl.ds(row, 1), :]) * (jnp.exp(att - cum) - jnp.exp(-cum))
+        heating = (wet_row(row) * light[pl.ds(row, 1), :]) * (jnp.exp(att - cum) - jnp.exp(-cum))
         heat_out[spot(row), :] = heating
         oc_out[2, spot(row), :] = oc_out[2, spot(row), :] + time_step * heating
 
     loop(ny, 4, heat)
-
-    def fold(t):
-        tr_out[t] = plain[t].astype(BF16)
-
-    loop(ntr, 2, fold)
+    results[2].start()
+    results[5].start()
 
     for index, (dy, dx) in enumerate(DIRS):
         @pl.when(has(dy, dx))
@@ -473,18 +500,22 @@
             def _(side=side):
                 for t in range(ntr):
                     forward_copy(side, t).wait_send()
-
-
-def expand_mask(wet_blocks):
-    blocks = wet_blocks.astype(F32)
-    rows, cols = blocks.shape
-    wide = jnp.broadcast_to(blocks[:, None, :, None], (rows, WBY, cols, WBX))
-    return wide.reshape(rows * WBY, cols * WBX)
+    for copy in results:
+        copy.wait()
+
+
+def hand_out(*refs):
+    count = len(refs) // 2
+    copies = [pltpu.make_async_copy(refs[k], refs[count + k], refs[-1].at[k]) for k in range(count)]
+    for copy in copies:
+        copy.start()
+    for copy in copies:
+        copy.wait()
 
 
 def shards(ngrp, ntile, ocean, tracers, wet_blocks, surface_light, rates):
     ntr, nz, ny, nx = tracers.shape
-    vmem = pl.BlockSpec(memory_space=pltpu.VMEM)
+    hbm = pl.BlockSpec(memory_space=pltpu.HBM)
     level, flat = (nz, nx), (nz * ny, nx)
     outs = pl.pallas_call(
         functools.partial(kernel, ngrp, ntile, ny),
@@ -493,9 +524,19 @@
             jax.ShapeDtypeStruct((ntr,) + flat, BF16),
             jax.ShapeDtypeStruct(flat, F32),
         ),
-        in_specs=[vmem] * 4 + [pl.BlockSpec(memory_space=pltpu.SMEM)],
-        out_specs=(vmem,) * 3,
+        in_specs=[hbm] * 5,
+        out_specs=(hbm,) * 3,
         scratch_shapes=[
+            pltpu.VMEM((4,) + flat, F32),
+            pltpu.VMEM((ntr,) + flat, BF16),
+            pltpu.VMEM(flat, F32),
+            pltpu.SemaphoreType.DMA((6,)),
+            pltpu.VMEM((ntr,) + flat, BF16),
+            pltpu.VMEM((4,) + flat, F32),
+            pltpu.SMEM(wet_blocks.shape, jnp.int32),
+            pltpu.VMEM(surface_light.shape, F32),
+            pltpu.SMEM(rates.shape, F32),
+            pltpu.SemaphoreType.DMA((5,)),
             pltpu.VMEM((2, ntr) + flat, BF16),
             pltpu.VMEM((2, len(RIM)) + level, BF16),
             pltpu.VMEM((2, len(RIM)) + level, BF16),
@@ -524,9 +565,17 @@
             pltpu.SemaphoreType.DMA((ntr,)),
         ],
         compiler_params=pltpu.CompilerParams(
-            collective_id=0, has_side_effects=True, vmem_limit_bytes=24 * 1024 * 1024
+            collective_id=0, has_side_effects=True, vmem_limit_bytes=VMEM_GRANT
         ),
-    )(tracers.reshape((ntr,) + flat), ocean.reshape((4,) + flat), expand_mask(wet_blocks), surface_light, rates)
+    )(tracers.reshape((ntr,) + flat), ocean.reshape((4,) + flat), wet_blocks, surface_light, rates)
+    outs = pl.pallas_call(
+        hand_out,
+        out_shape=[jax.ShapeDtypeStruct(out.shape, out.dtype) for out in outs],
+        in_specs=[hbm] * 3,
+        out_specs=[hbm] * 3,
+        scratch_shapes=[pltpu.SemaphoreType.DMA((3,))],
+        compiler_params=pltpu.CompilerParams(vmem_limit_bytes=VMEM_GRANT),
+    )(*outs)
     return outs[0].reshape(ocean.shape), outs[1].reshape(tracers.shape), outs[2].reshape(ocean.shape[1:])
 
 

time: 30.7 us -> 46.9 us (1.53)
  Pallas kernels: 24.3 us -> 46.2 us
  local copies, waits for them, and re-layouts: 5.45 us -> 0 us
    pallas_call x0 -> x1, Pallas kernels: none -> 21 us  [shards(): pl.pallas_call(hand_out, out_shape=[jax.ShapeDtypeStruct(out.shape, out.d...]
    unnamed x13 -> x0, local copies, waits for them, and re-layouts: 5.29 us -> none
    pallas_call x1, Pallas kernels: 24.3 us -> 25.2 us  [shards(): pl.pallas_call(functools.partial(kernel, ngrp, ntile, ny), out_shape=(jax...]
where the time goes in v4:
time: 46.9 us; the launch traced here: 46.8 us
  Pallas kernels  46.2 us (99%)
  between operations  0.64 us (1%)
    pallas_call x1, Pallas kernels, shards(): pl.pallas_call(functools.partial(kernel, ngrp, ntile, ny), out_shape=(jax...  25.2 us
    pallas_call x1, Pallas kernels, shards(): pl.pallas_call(hand_out, out_shape=[jax.ShapeDtypeStruct(out.shape, out.d...  21 us

profile of v4, /device:TPU:1, one launch (start us, length us, event | category | flops | bytes accessed | tf_op | source)
XLA Modules:
  0.0 46.8 jit_solution(6846683204424508884)
XLA Ops:
  0.6 25.2 %shard_map.76 = (f32[4,128,128]{2,1,0:T(8,128)}, bf16[10,128,128]{2,1,0:T(8,128)(2,1)}, f32[128,128]{1,0:T(8,128)}) custom-call(bf16[10,128,128]{2,1,0:T(8,128)(2,1)} %bitcast.5, f32[4,128,128]{2,1,0:T(8,128)} %bitcast.6, s32[1,8]{1,0:T(1,128)} %wet_in.1, f32[4,128]{1,0:T(4,128)} %light_in.1, f32[10,10]{1,0:T(8,128)} %rates_in.1), custom_call_target="tpu_custom_call" | custom-call | tf_op jit(solution)/shard_map/pallas_call | solution.py:520
  25.8 21.0 %shard_map.77 = (f32[4,128,128]{2,1,0:T(8,128)}, bf16[10,128,128]{2,1,0:T(8,128)(2,1)}, f32[128,128]{1,0:T(8,128)}) custom-call(f32[4,128,128]{2,1,0:T(8,128)} %get-tuple-element.9.refs_0_, bf16[10,128,128]{2,1,0:T(8,128)(2,1)} %get-tuple-element.10.refs_1_, f32[128,128]{1,0:T(8,128)} %get-tuple-element.11.refs_2_), custom_call_target="tpu_custom_call" | custom-call | tf_op jit(solution)/shard_map/pallas_call | solution.py:571

commit v5 on v4

--- a/solution.py
+++ b/solution.py
@@ -181,11 +181,25 @@
         @pl.when(there[2 * side - 1])
         def _(side=side):
             ocean_copy(side).start()
-    for t in range(ntr):
+    def launch(t):
         for side in (0, 1):
             @pl.when(sends(side))
-            def _(side=side, t=t):
+            def _(side=side):
                 tracer_copy(side, t).start()
+
+    in_flight = min(3, ntr)
+    pumped = min(7, ntr - in_flight)
+
+    def pump(t):
+        if t < pumped:
+            for side in (0, 1):
+                @pl.when(sends(side))
+                def _(side=side):
+                    tracer_copy(side, t).wait_send()
+            launch(t + in_flight)
+
+    for t in range(in_flight):
+        launch(t)
 
     for index, (dy, dx) in enumerate(DIRS):
         @pl.when(jnp.logical_not(has(-dy, -dx)))
@@ -202,6 +216,7 @@
         @pl.when(has(-dy, -dx))
         def _(dy=dy, dx=dx, index=index):
             edge_copy(dy, dx, index).wait_recv()
+    pump(0)
 
     part = lane % GROUP
     near_west = part == GROUP // 2
@@ -228,6 +243,7 @@
         z1[slot] = mid + 0.5 * minmod(mid - far, close - mid)
 
     loop(ny + 4, 4, strips)
+    pump(1)
     forward(0)
 
     blend = jnp.where(group < ntr + 2, viscosity, diffusion)
@@ -275,8 +291,9 @@
         z2[row] = mid + 0.5 * minmod(mid - far, close - mid)
 
     loop(ny, 4, strip_row)
-    for t in (1, 2):
-        forward(t)
+    pump(2)
+    forward(1)
+    pump(3)
 
     for side in (0, 1):
         @pl.when(there[1 - 2 * side])
@@ -320,7 +337,8 @@
             o1[f, k] = keep * (oe[f, k + 2] + time_step * rate[f])
 
     loop(ny + 2, 3, ocean_first)
-    for t in (3, 4):
+    pump(4)
+    for t in (2, 3):
         forward(t)
 
     def ocean_second(row):
@@ -334,7 +352,8 @@
     results.append(pltpu.make_async_copy(heat_out, heat_final, out_sem.at[5]))
     for f in (0, 1, 3):
         results[f].start()
-    forward(5)
+    pump(5)
+    forward(4)
 
     def zonal_faces(scale, mid, edge):
         rim = lanes(edge, shift_back(ntr))
@@ -364,8 +383,9 @@
 
     loop(ny + 1, 5, merid_second)
 
-    forward(6)
-    ahead = 7
+    pump(6)
+    forward(5)
+    ahead = 6
     chunk = 16
     clane = lane_of((chunk, nx))
     cfirst, clast = clane == 0, clane == nx - 1
@@ -492,7 +512,7 @@
 
         @pl.when(sends(side))
         def _(side=side):
-            for t in range(ntr):
+            for t in range(pumped, ntr):
                 tracer_copy(side, t).wait_send()
 
         if relay:
@@ -504,12 +524,20 @@
         copy.wait()
 
 
-def hand_out(*refs):
-    count = len(refs) // 2
-    copies = [pltpu.make_async_copy(refs[k], refs[count + k], refs[-1].at[k]) for k in range(count)]
-    for copy in copies:
+def hand_out(ocean, tracers, heat, ocean_out, tracers_out, heat_out, ocean_held, tracers_held, heat_held, in_sem, out_sem):
+    pieces = [(ocean.at[f], ocean_held.at[f], ocean_out.at[f]) for f in range(ocean.shape[0])]
+    pieces += [(heat, heat_held, heat_out)]
+    half = tracers.shape[0] // 2
+    for part in (pl.ds(0, half), pl.ds(half, tracers.shape[0] - half)):
+        pieces.append((tracers.at[part], tracers_held.at[part], tracers_out.at[part]))
+    loads = [pltpu.make_async_copy(p[0], p[1], in_sem.at[k]) for k, p in enumerate(pieces)]
+    stores = [pltpu.make_async_copy(p[1], p[2], out_sem.at[k]) for k, p in enumerate(pieces)]
+    for copy in loads:
         copy.start()
-    for copy in copies:
+    for load, store in zip(loads, stores):
+        load.wait()
+        store.start()
+    for copy in stores:
         copy.wait()
 
 
@@ -573,7 +601,7 @@
         out_shape=[jax.ShapeDtypeStruct(out.shape, out.dtype) for out in outs],
         in_specs=[hbm] * 3,
         out_specs=[hbm] * 3,
-        scratch_shapes=[pltpu.SemaphoreType.DMA((3,))],
+        scratch_shapes=[pltpu.VMEM(out.shape, out.dtype) for out in outs] + [pltpu.SemaphoreType.DMA((7,))] * 2,
         compiler_params=pltpu.CompilerParams(vmem_limit_bytes=VMEM_GRANT),
     )(*outs)
     return outs[0].reshape(ocean.shape), outs[1].reshape(tracers.shape), outs[2].reshape(ocean.shape[1:])

time: 46.9 us -> 27.2 us (0.58)
  Pallas kernels: 46.2 us -> 26.4 us
    pallas_call x1, Pallas kernels: 21 us -> 1.95 us  [shards(): pl.pallas_call(hand_out, out_shape=[jax.ShapeDtypeStruct(out.shape, out.d...]
    pallas_call x1, Pallas kernels: 25.2 us -> 24.5 us  [shards(): pl.pallas_call(functools.partial(kernel, ngrp, ntile, ny), out_shape=(jax...]
where the time goes in v5:
time: 27.2 us; the launch traced here: 27 us
  Pallas kernels  26.4 us (97%)
  between operations  0.64 us (2%)
    pallas_call x1, Pallas kernels, shards(): pl.pallas_call(functools.partial(kernel, ngrp, ntile, ny), out_shape=(jax...  24.5 us
    pallas_call x1, Pallas kernels, shards(): pl.pallas_call(hand_out, out_shape=[jax.ShapeDtypeStruct(out.shape, out.d...  1.95 us

profile of v5, /device:TPU:1, one launch (start us, length us, event | category | flops | bytes accessed | tf_op | source)
XLA Modules:
  0.0 27.0 jit_solution(13745538164260590769)
XLA Ops:
  0.6 24.5 %shard_map.76 = (f32[4,128,128]{2,1,0:T(8,128)}, bf16[10,128,128]{2,1,0:T(8,128)(2,1)}, f32[128,128]{1,0:T(8,128)}) custom-call(bf16[10,128,128]{2,1,0:T(8,128)(2,1)} %bitcast.5, f32[4,128,128]{2,1,0:T(8,128)} %bitcast.6, s32[1,8]{1,0:T(1,128)} %wet_in.1, f32[4,128]{1,0:T(4,128)} %light_in.1, f32[10,10]{1,0:T(8,128)} %rates_in.1), custom_call_target="tpu_custom_call" | custom-call | tf_op jit(solution)/shard_map/pallas_call | solution.py:548
  25.1 1.9 %shard_map.77 = (f32[4,128,128]{2,1,0:T(8,128)}, bf16[10,128,128]{2,1,0:T(8,128)(2,1)}, f32[128,128]{1,0:T(8,128)}) custom-call(f32[4,128,128]{2,1,0:T(8,128)} %get-tuple-element.9.ocean, bf16[10,128,128]{2,1,0:T(8,128)(2,1)} %get-tuple-element.10.tracers, f32[128,128]{1,0:T(8,128)} %get-tuple-element.11.heat), custom_call_target="tpu_custom_call" | custom-call | tf_op jit(solution)/shard_map/pallas_call | solution.py:599

commit v6 on v5

--- a/solution.py
+++ b/solution.py
@@ -386,8 +386,8 @@
     pump(6)
     forward(5)
     ahead = 6
-    chunk = 16
-    clane = lane_of((chunk, nx))
+    thin = 8
+    clane = lane_of((thin, nx))
     cfirst, clast = clane == 0, clane == nx - 1
 
     def zonal_part(c, rim, rim_value, speeds):
@@ -399,14 +399,23 @@
         after = jnp.where(clast, rim_value, lanes(right, -1))
         return (speeds[2] * left + speeds[3] * after) - (speeds[0] * before + speeds[1] * right)
 
-    def merid_part(c, speeds):
-        d = [b - a for a, b in zip(c[:-1], c[1:])]
-        h = [0.5 * minmod(a, b) for a, b in zip(d[:-1], d[1:])]
-        flux = []
-        for k in range(len(h) - 1):
-            plus, minus = speeds(k)
-            flux.append(plus * (c[k + 1] + h[k]) + minus * (c[k + 2] - h[k + 1]))
-        return [b - a for a, b in zip(flux[:-1], flux[1:])]
+    def slide(values, take):
+        c, d, h, f = [], [None], [None], [None]
+
+        def push(x, speeds):
+            c.append(x)
+            i = len(c) - 1
+            if i >= 1:
+                d.append(c[i] - c[i - 1])
+            if i >= 2:
+                h.append(0.5 * minmod(d[i - 1], d[i]))
+            if i >= 3:
+                plus, minus = speeds(i - 3)
+                f.append(plus * (c[i - 2] + h[i - 2]) + minus * (c[i - 1] - h[i - 1]))
+            if i >= 4:
+                take(i - 4, c[i - 2], f[i - 2] - f[i - 3])
+
+        values(push)
 
     def tracer(t, carry):
         for side in (0, 1):
@@ -422,32 +431,43 @@
         back = nx - (GROUP * t + GROUP // 2)
 
         def levels(zc):
-            zs = pl.ds(zc * chunk, chunk)
-            c = [around[1, spot(k + ny - HALO, zc * chunk, chunk), :] for k in range(HALO)]
-            c += [plain[t, spot(k, zc * chunk, chunk), :] for k in range(ny)]
-            c += [around[0, spot(k, zc * chunk, chunk), :] for k in range(HALO)]
-            along_y = merid_part(c, lambda k: (va[0, k, zs], va[1, k, zs]))
-            one = []
-            for j in range(ny + 4):
-                rim = pltpu.roll(m1[j, zs], back, 1)
-                rim_value = pltpu.roll(z1[j, zs], back, 1)
-                mid = c[j + 2]
-                div = zonal_part(mid, rim, rim_value, [ua[k, j, zs] for k in range(4)]) + along_y[j]
-                new = (mid - div).astype(BF16).astype(F32)
-                if j < 2:
-                    new = in_south * new
-                if j >= ny + 2:
-                    new = in_north * new
-                one.append(new)
-            along_y = merid_part(one, lambda k: (vb[0, k, zs], vb[1, k, zs]))
-            for j in range(ny):
+            zs = pl.ds(zc * thin, thin)
+            start = []
+
+            def second(push):
+                def take(j, mid, along_y):
+                    rim = pltpu.roll(m1[j, zs], back, 1)
+                    rim_value = pltpu.roll(z1[j, zs], back, 1)
+                    div = zonal_part(mid, rim, rim_value, [ua[k, j, zs] for k in range(4)]) + along_y
+                    new = (mid - div).astype(BF16).astype(F32)
+                    if j < 2:
+                        new = in_south * new
+                    if j >= ny + 2:
+                        new = in_north * new
+                    push(new, lambda k: (vb[0, k, zs], vb[1, k, zs]))
+
+                def first(push_start):
+                    for i in range(ny + 2 * HALO):
+                        if i < HALO:
+                            x = around[1, spot(i + ny - HALO, zc * thin, thin), :]
+                        elif i < HALO + ny:
+                            x = plain[t, spot(i - HALO, zc * thin, thin), :]
+                        else:
+                            x = around[0, spot(i - HALO - ny, zc * thin, thin), :]
+                        start.append(x)
+                        push_start(x, lambda k: (va[0, k, zs], va[1, k, zs]))
+
+                slide(first, take)
+
+            def finish(j, mid, along_y):
                 rim = pltpu.roll(m2[j, zs], back, 1)
                 rim_value = pltpu.roll(z2[j, zs], back, 1)
-                mid = one[j + 2]
-                div = zonal_part(mid, rim, rim_value, [ub[k, j, zs] for k in range(4)]) + along_y[j]
-                tt[t, j, zs] = 0.5 * (c[j + 4] + mid) - div
-
-        for zc in range(nz // chunk):
+                div = zonal_part(mid, rim, rim_value, [ub[k, j, zs] for k in range(4)]) + along_y
+                tt[t, j, zs] = 0.5 * (start[j + HALO] + mid) - div
+
+            slide(second, finish)
+
+        for zc in range(nz // thin):
             levels(zc)
         if relay:
             @pl.when(t + ahead < ntr)
@@ -459,6 +479,7 @@
 
     for copy in inputs[2:]:
         copy.wait()
+    chunk = 16
     block = lane_of((1, nx)) // WBX
 
     def wet_row(row):

time: 27.2 us -> 27.1 us (level)
  no operation moved by 1% of the time
where the time goes in v6:
time: 27.1 us; the launch traced here: 26.9 us
  Pallas kernels  26.3 us (97%)
  between operations  0.64 us (2%)
    pallas_call x1, Pallas kernels, shards(): pl.pallas_call(functools.partial(kernel, ngrp, ntile, ny), out_shape=(jax...  24.3 us
    pallas_call x1, Pallas kernels, shards(): pl.pallas_call(hand_out, out_shape=[jax.ShapeDtypeStruct(out.shape, out.d...  1.95 us

profile of v6, /device:TPU:1, one launch (start us, length us, event | category | flops | bytes accessed | tf_op | source)
XLA Modules:
  0.0 26.9 jit_solution(3394590045140150726)
XLA Ops:
  0.6 24.3 %shard_map.76 = (f32[4,128,128]{2,1,0:T(8,128)}, bf16[10,128,128]{2,1,0:T(8,128)(2,1)}, f32[128,128]{1,0:T(8,128)}) custom-call(bf16[10,128,128]{2,1,0:T(8,128)(2,1)} %bitcast.5, f32[4,128,128]{2,1,0:T(8,128)} %bitcast.6, s32[1,8]{1,0:T(1,128)} %wet_in.1, f32[4,128]{1,0:T(4,128)} %light_in.1, f32[10,10]{1,0:T(8,128)} %rates_in.1), custom_call_target="tpu_custom_call" | custom-call | tf_op jit(solution)/shard_map/pallas_call | solution.py:569
  24.9 1.9 %shard_map.77 = (f32[4,128,128]{2,1,0:T(8,128)}, bf16[10,128,128]{2,1,0:T(8,128)(2,1)}, f32[128,128]{1,0:T(8,128)}) custom-call(f32[4,128,128]{2,1,0:T(8,128)} %get-tuple-element.9.ocean, bf16[10,128,128]{2,1,0:T(8,128)(2,1)} %get-tuple-element.10.tracers, f32[128,128]{1,0:T(8,128)} %get-tuple-element.11.heat), custom_call_target="tpu_custom_call" | custom-call | tf_op jit(solution)/shard_map/pallas_call | solution.py:620
